TPU v7x, 32 devices: a whole 2x2x4 slice. The times are simulated.
32 devices in a mesh: seq: 8 (over z, x), batch: 4 (over y, core).
Axes of the slice: x: 2, y: 2, z: 4, core: 2. Of those that a mesh axis runs over, the one named last changes fastest.
Arguments:
- inputs: bfloat16 [4, 1024, 768], P('batch', 'seq'), may hold values from -6 to 6
- cotangent: bfloat16 [4, 1024, 768], P('batch', 'seq'), may hold values from -6 to 6
- doc_lengths: int32 [4, 9], P('batch'), may hold values from 1 to 896, as said below
- gain_one: float32 [768], replicated, may hold values from 0.5 to 1.5
- shift_one: float32 [768], replicated, may hold values from -2 to 2
- qkv_weight: bfloat16 [768, 2304], replicated, may hold values from -0.21875 to 0.21875
- qkv_bias: float32 [2304], replicated, may hold values from -2 to 2
- proj_weight: bfloat16 [768, 768], replicated, may hold values from -6 to 6
- proj_bias: float32 [768], replicated, may hold values from -2 to 2
- gain_two: float32 [768], replicated, may hold values from 0.5 to 1.5
- shift_two: float32 [768], replicated, may hold values from -2 to 2
- up_weight: bfloat16 [768, 3072], replicated, may hold values from -0.21875 to 0.21875
- up_bias: float32 [3072], replicated, may hold values from -2 to 2
- down_weight: bfloat16 [3072, 768], replicated, may hold values from -0.109375 to 0.109375
- down_bias: float32 [768], replicated, may hold values from -2 to 2
Outputs:
- layer_out: bfloat16 [4, 1024, 768], P('batch', 'seq')
- input_grad: bfloat16 [4, 1024, 768], P('batch', 'seq')
- grad_gain_one: float32 [768], replicated
- grad_shift_one: float32 [768], replicated
- grad_qkv_weight: float32 [768, 2304], replicated
- grad_qkv_bias: float32 [2304], replicated
- grad_proj_weight: float32 [768, 768], replicated
- grad_proj_bias: float32 [768], replicated
- grad_gain_two: float32 [768], replicated
- grad_shift_two: float32 [768], replicated
- grad_up_weight: float32 [768, 3072], replicated
- grad_up_bias: float32 [3072], replicated
- grad_down_weight: float32 [3072, 768], replicated
- grad_down_bias: float32 [768], replicated
Inputs may be any that keep to these rules, and one draw needn't show every extreme that they name: `doc_lengths`: each row lists in order the lengths of the 9 documents packed into one stream: 8 short ones that hold 128 tokens together, and one of exactly 896 tokens with at least one short document before it and one after it.
All inputs are finite; a program needn't handle non-finite values.
Results may differ from a plain program's by a relative error of at most 0.018.
Values may be sent and summed in bfloat16 or wider, within the bound.
A program may use at most 256 MiB of HBM per device.

v0:
```python
import math

import jax
import jax.numpy as jnp
from jax import lax
from jax.sharding import PartitionSpec as P

HEADS = 12
HD = 64


norm_eps = 1e-05
masked_low = -1e30


def from_behind(shard, axis, by):
    peers = lax.axis_size(axis)
    pairs = [(i, i + by) for i in range(peers) if 0 <= i + by < peers]
    return lax.ppermute(shard, axis, pairs)


def shifted(block, axis, distance):
    devices = range(lax.axis_size(axis))
    route = [((i - distance) % len(devices), i) for i in devices]
    return lax.ppermute(block, axis, route)


def layer_norm(rows, gain, shift):
    center = rows - jnp.mean(rows, axis=-1, keepdims=True)
    spread = jnp.mean(center * center, axis=-1, keepdims=True)
    return center * lax.rsqrt(spread + norm_eps) * gain + shift


def gelu_tanh(value):
    return jax.nn.gelu(value, approximate=True)


def doc_of(ends, first, count):
    places = first + jnp.arange(count, dtype=jnp.int32)
    return jnp.sum((ends[None, :] <= places[:, None]).astype(jnp.int32), axis=1)


def scores_of(q_heads, k_heads, allowed):
    raw = jnp.einsum("qhd,khd->hqk", q_heads, k_heads, preferred_element_type=jnp.float32)
    return jnp.where(allowed[None], raw * (1.0 / math.sqrt(q_heads.shape[2])), 0.0)


def forward_part(state, q_heads, k_heads, v_heads, allowed):
    running, total, accum = state
    scores = scores_of(q_heads, k_heads, allowed)
    top = jnp.max(jnp.where(allowed[None], jnp.abs(scores), masked_low), axis=2)
    newer = jnp.maximum(running, top)
    plus = jnp.where(allowed[None], jnp.exp(scores - newer[:, :, None]), 0.0)
    minus = jnp.where(allowed[None], jnp.exp(-scores - newer[:, :, None]), 0.0)
    keep = jnp.exp(running - newer)
    total = total * keep + jnp.sum(plus + minus, axis=2)
    weights = (plus - minus).astype(jnp.bfloat16)
    accum = accum * keep[:, :, None] + jnp.einsum(
        "hqk,khd->hqd", weights, v_heads, preferred_element_type=jnp.float32
    )
    return (newer, total, accum)


def backward_part(q_heads, k_heads, v_heads, grad_out, log_total, delta, allowed):
    scale = 1.0 / math.sqrt(q_heads.shape[2])
    scores = scores_of(q_heads, k_heads, allowed)
    plus = jnp.where(allowed[None], jnp.exp(scores - log_total[:, :, None]), 0.0)
    minus = jnp.where(allowed[None], jnp.exp(-scores - log_total[:, :, None]), 0.0)
    signed = plus - minus
    along = jnp.einsum("qhd,khd->hqk", grad_out, v_heads, preferred_element_type=jnp.float32)
    dscore = (((plus + minus) * along - signed * delta[:, :, None]) * scale).astype(jnp.bfloat16)
    weights = signed.astype(jnp.bfloat16)
    grad_q = jnp.einsum("hqk,khd->qhd", dscore, k_heads, preferred_element_type=jnp.float32)
    grad_k = jnp.einsum("hqk,qhd->khd", dscore, q_heads, preferred_element_type=jnp.float32)
    grad_v = jnp.einsum("hqk,qhd->khd", weights, grad_out, preferred_element_type=jnp.float32)
    return (grad_q, grad_k, grad_v)


def forward_step(state, q_heads, k_heads, v_heads, allowed):
    return forward_part(state, q_heads, k_heads, v_heads, allowed)


def backward_step(q_heads, k_heads, v_heads, grad_out, log_total, delta, allowed):
    return backward_part(q_heads, k_heads, v_heads, grad_out, log_total, delta, allowed)


def per_device(
    inputs,
    cotangent,
    doc_lengths,
    gain_one,
    shift_one,
    qkv_weight,
    qkv_bias,
    proj_weight,
    proj_bias,
    gain_two,
    shift_two,
    up_weight,
    up_bias,
    down_weight,
    down_bias,
):
    rows = inputs.shape[1]
    width = inputs.shape[2]
    index = lax.axis_index("seq")
    count = lax.axis_size("seq")
    ends = jnp.cumsum(doc_lengths[0])
    q_place = index * rows + jnp.arange(rows, dtype=jnp.int32)
    q_doc = doc_of(ends, index * rows, rows)

    def heads(flat):
        return flat.reshape(flat.shape[0], HEADS, HD)

    x_rows = inputs[0].astype(jnp.float32)
    norm_one = layer_norm(x_rows, gain_one, shift_one).astype(jnp.bfloat16)
    mixed = (jnp.dot(norm_one, qkv_weight, preferred_element_type=jnp.float32) + qkv_bias).astype(
        jnp.bfloat16
    )
    q_flat = mixed[:, :width]
    k_flat = mixed[:, width : 2 * width]
    v_flat = mixed[:, 2 * width :]
    q_heads = heads(q_flat)

    def allowed_for(first, extent):
        k_place = first + jnp.arange(extent, dtype=jnp.int32)
        k_doc = doc_of(ends, first, extent)
        return (q_doc[:, None] == k_doc[None, :]) & (k_place[None, :] <= q_place[:, None])

    start_state = (
        jnp.full((HEADS, rows), masked_low, jnp.float32),
        jnp.zeros((HEADS, rows), jnp.float32),
        jnp.zeros((HEADS, rows, HD), jnp.float32),
    )
    state = start_state
    k_all = lax.all_gather(k_flat, "seq", axis=0, tiled=True)
    v_all = lax.all_gather(v_flat, "seq", axis=0, tiled=True)
    fold_extent = k_all.shape[0]
    number = fold_extent // rows

    def one(inner, block):
        offset = block * rows
        k_blk = lax.dynamic_slice_in_dim(k_all, offset, rows, 0)
        v_blk = lax.dynamic_slice_in_dim(v_all, offset, rows, 0)
        allowed = allowed_for(offset, rows)
        return (forward_step(inner, q_heads, heads(k_blk), heads(v_blk), allowed), None)

    state, unused = lax.scan(one, state, jnp.arange(number, dtype=jnp.int32))
    running, total, accum = state
    attn_heads = accum / total[:, :, None]
    attn32 = jnp.transpose(attn_heads, (1, 0, 2)).reshape(rows, width)
    attn = attn32.astype(jnp.bfloat16)
    resid = x_rows + jnp.dot(attn, proj_weight, preferred_element_type=jnp.float32) + proj_bias
    norm_two = layer_norm(resid, gain_two, shift_two).astype(jnp.bfloat16)
    hidden = jnp.dot(norm_two, up_weight, preferred_element_type=jnp.float32) + up_bias
    active = gelu_tanh(hidden).astype(jnp.bfloat16)
    result = resid + jnp.dot(active, down_weight, preferred_element_type=jnp.float32) + down_bias
    layer_out = result.astype(jnp.bfloat16)[None]
    grad_rows = cotangent[0]
    grad_down_weight = jnp.einsum(
        "tf,td->fd", active, grad_rows, preferred_element_type=jnp.float32
    )
    grad_down_bias = jnp.sum(grad_rows.astype(jnp.float32), axis=0)
    grad_active = jnp.dot(grad_rows, down_weight.T, preferred_element_type=jnp.float32)
    gelu_back = jax.vjp(gelu_tanh, hidden)[1]
    grad_hidden = gelu_back(grad_active)[0].astype(jnp.bfloat16)
    grad_up_weight = jnp.einsum(
        "td,tf->df", norm_two, grad_hidden, preferred_element_type=jnp.float32
    )
    grad_up_bias = jnp.sum(grad_hidden.astype(jnp.float32), axis=0)
    grad_norm_two = jnp.dot(grad_hidden, up_weight.T, preferred_element_type=jnp.float32)
    norm_two_back = jax.vjp(layer_norm, resid, gain_two, shift_two)[1]
    resid_part, grad_gain_two, grad_shift_two = norm_two_back(grad_norm_two)
    grad_resid = grad_rows.astype(jnp.float32) + resid_part
    grad_branch = grad_resid.astype(jnp.bfloat16)
    grad_proj_weight = jnp.einsum(
        "td,te->de", attn, grad_branch, preferred_element_type=jnp.float32
    )
    grad_proj_bias = jnp.sum(grad_branch.astype(jnp.float32), axis=0)
    grad_attn = jnp.dot(grad_branch, proj_weight.T, preferred_element_type=jnp.float32).astype(
        jnp.bfloat16
    )
    grad_out = heads(grad_attn)
    log_total = running + jnp.log(total)
    delta = jnp.einsum("qhd,hqd->hq", grad_out.astype(jnp.float32), attn_heads)

    def circle_step(step, carry):
        k_held, v_held, acc_k, acc_v, grad_q = carry
        source = jnp.remainder(index - step, count)
        allowed = allowed_for(source * rows, rows)
        part = backward_step(
            q_heads, heads(k_held), heads(v_held), grad_out, log_total, delta, allowed
        )
        grad_q = grad_q + part[0]
        acc_k = acc_k + part[1].reshape(rows, width)
        acc_v = acc_v + part[2].reshape(rows, width)
        k_held, v_held = from_behind((k_held, v_held), "seq", 1)
        acc_k, acc_v = (
            shifted(acc_k.astype(jnp.bfloat16), "seq", 1).astype(acc_k.dtype),
            shifted(acc_v.astype(jnp.bfloat16), "seq", 1).astype(acc_v.dtype),
        )
        return (k_held, v_held, acc_k, acc_v, grad_q)

    circle_start = (
        k_flat,
        v_flat,
        jnp.zeros((rows, width), jnp.float32),
        jnp.zeros((rows, width), jnp.float32),
        jnp.zeros((rows, HEADS, HD), jnp.float32),
    )
    unused_k, unused_v, grad_k, grad_v, grad_q = lax.fori_loop(0, count, circle_step, circle_start)
    grad_mixed = jnp.concatenate(
        [
            grad_q.reshape(rows, width).astype(jnp.bfloat16),
            grad_k.astype(jnp.bfloat16),
            grad_v.astype(jnp.bfloat16),
        ],
        axis=1,
    )
    grad_qkv_weight = jnp.einsum(
        "td,te->de", norm_one, grad_mixed, preferred_element_type=jnp.float32
    )
    grad_qkv_bias = jnp.sum(grad_mixed.astype(jnp.float32), axis=0)
    grad_norm_one = jnp.dot(grad_mixed, qkv_weight.T, preferred_element_type=jnp.float32)
    norm_one_back = jax.vjp(layer_norm, x_rows, gain_one, shift_one)[1]
    input_part, grad_gain_one, grad_shift_one = norm_one_back(grad_norm_one)
    input_grad = (grad_resid + input_part).astype(jnp.bfloat16)[None]
    members = (
        grad_gain_one,
        grad_shift_one,
        grad_qkv_weight,
        grad_qkv_bias,
        grad_proj_weight,
        grad_proj_bias,
        grad_gain_two,
        grad_shift_two,
        grad_up_weight,
        grad_up_bias,
        grad_down_weight,
        grad_down_bias,
    )
    joined = jnp.concatenate([member.reshape(-1) for member in members])
    summed = lax.psum_scatter(joined, ("seq", "batch"), scatter_dimension=0, tiled=True)
    whole = lax.all_gather(
        summed.astype(jnp.bfloat16), ("seq", "batch"), axis=0, tiled=True
    ).astype(summed.dtype)
    outputs = []
    offset = 0
    for member in members:
        extent = member.size
        outputs.append(whole[offset : offset + extent].reshape(member.shape))
        offset = offset + extent
    return (
        layer_out,
        input_grad,
        outputs[0],
        outputs[1],
        outputs[2],
        outputs[3],
        outputs[4],
        outputs[5],
        outputs[6],
        outputs[7],
        outputs[8],
        outputs[9],
        outputs[10],
        outputs[11],
    )


def solution(mesh):
    in_specs = (
        P("batch", "seq", None),
        P("batch", "seq", None),
        P("batch", None),
        P(),
        P(),
        P(),
        P(),
        P(),
        P(),
        P(),
        P(),
        P(),
        P(),
        P(),
        P(),
    )
    out_specs = (
        P("batch", "seq", None),
        P("batch", "seq", None),
        P(),
        P(),
        P(),
        P(),
        P(),
        P(),
        P(),
        P(),
        P(),
        P(),
        P(),
        P(),
    )
    return jax.shard_map(
        per_device, mesh=mesh, in_specs=in_specs, out_specs=out_specs, check_vma=False
    )
```

profile of v0, /device:TPU:0, one launch (start us, length us, event | category | flops | bytes accessed | tf_op | source)
XLA Modules:
  0.0 1429.9 jit_solution(15000022725188257302)
XLA Ops:
  20.7 38.8 %all-gather.3.cloned.1.call-done = bf16[1024,768]{1,0:T(8,128)(2,1)} async-done(((bf16[128,768]{1,0:T(8,128)(2,1)}), bf16[1024,768]{1,0:T(8,128)(2,1)}) %all-gather.3.cloned.1.call-update) | async-done | bytes 1572880 | tf_op jit(solution)/shard_map/all_gather | solution.py:136
  59.4 45.8 %all-gather.5.cloned.1.call-done = bf16[1024,768]{1,0:T(8,128)(2,1)} async-done(((bf16[128,768]{1,0:T(8,128)(2,1)}), bf16[1024,768]{1,0:T(8,128)(2,1)}) %all-gather.5.cloned.1.call-update) | async-done | bytes 1572880 | tf_op jit(solution)/shard_map/all_gather | solution.py:137
  105.7 144.0 %while.39 = (s32[]{:T(128)}, f32[12,128]{1,0:T(8,128)}, f32[12,128]{1,0:T(8,128)}, f32[12,128,64]{1,2,0:T(8,128)}, s32[128]{0:T(128)}, /*index=5*/s32[9]{0:T(128...) while((s32[]{:T(128)}, f32[12,128]{1,0:T(8,128)}, ...), condition=%wide.region_8.9_spmd.clone, body=%wide.region_4.8_spmd.clone.sunk | while | flops 54422532 | bytes 5542175 | solution.py:148
  256.4 5.5 convert_reduce_fusion.2
  272.0 215.4 %while.40 = (s32[]{:T(128)}, bf16[128,768]{0,1:T(8,128)(2,1)}, bf16[128,768]{0,1:T(8,128)(2,1)}, f32[128,768]{0,1:T(8,128)}, f32[128,768]{0,1:T(8,128)}, /*index...) while((s32[]{:T(128)}, bf16[128,768]{0,1:T(8,128)(2,1)}, ...), condition=%wide.region_15.16_spmd.clone, body=%wide.region_13.15_spmd.clone.sunk | while | flops 130993680 | bytes 19995340 | solution.py:211
  278.3 4.7 collective-permute-start.1
  293.7 5.5 collective-permute-done.2
  321.9 3.9 collective-permute-done.2
  347.6 4.5 collective-permute-done.2
  386.5 3.6 collective-permute-start.1
  413.4 3.6 collective-permute-start.1
  427.4 3.9 collective-permute-done.2
  493.2 4.2 fusion.60
  499.6 5.3 convolution_bitcast_fusion.1
  504.8 5.2 fusion.51
  510.6 7.9 reshape.357
  520.9 9.6 copy.69
  530.5 10.8 reshape.360
  547.7 60.7 %dynamic-update-slice.3 = f32[7087872]{0:T(1024)} dynamic-update-slice(f32[7087872]{0:T(1024)} %constant_dynamic-update-slice_fusion.8, f32[1769472]{0:T(1024)} %reshape.357, s32[]{} %constant.149) | dynamic-update-slice | bytes 14155780
  609.7 20.3 %dynamic-update-slice.5 = f32[7087872]{0:T(1024)} dynamic-update-slice(f32[7087872]{0:T(1024)} %constant_dynamic-update-slice_fusion.7, f32[589824]{0:T(1024)S(1)} %reshape.358, s32[]{} %constant.151) | dynamic-update-slice | bytes 4718596
  633.9 9.3 constant_dynamic-update-slice_fusion.3
  643.8 3.9 constant_dynamic-update-slice_fusion.1
  648.4 457.8 %all-reduce.6 = bf16[7087872]{0:T(1024)(128)(2,1)} all-reduce(f32[7087872]{0:T(1024)} %constant_dynamic-update-slice_fusion), channel_id=2, replica_groups=mesh['seq'=8,'batch'=4] {'seq','batch'}, use_global_device_ids=true, to_apply=%region_26.27.clone | all-reduce | flops 7087872 | bytes 42527232
  1107.4 5.2 broadcast.252
  1112.7 7.6 dynamic-update-slice
  1121.6 4.1 fusion.35
  1125.7 242.6 %all-reduce.5.cloned.1.call-done = bf16[7087872]{0:T(1024)(128)(2,1)} async-done(((bf16[7087872]{0:T(1024)(128)(2,1)}), bf16[7087872]{0:T(1024)(128)(2,1)}) %all-reduce.5.cloned.1.call-update) | async-done | bytes 14175760
  1368.3 9.6 fusion.69
  1377.9 10.9 reshape.362
  1388.8 11.3 slice.80
  1400.1 4.7 slice.87
  1404.7 8.2 reshape.361
  (583 shorter events, 390.3 us)
Async XLA Ops:
  7.2 52.3 %all-gather.3.cloned.1.call-start = ((), (), s32[]{:S(2)}) async-start(), calls=%async_computation | async-start | bytes 1769472 | tf_op jit(solution)/shard_map/all_gather | solution.py:136
  12.6 92.6 %all-gather.5.cloned.1.call-start = ((), (), s32[]{:S(2)}) async-start(), calls=%async_computation.1 | async-start | bytes 1769472 | tf_op jit(solution)/shard_map/all_gather | solution.py:137
  13.4 1354.9 %all-reduce.5.cloned.1.call-start = ((), (), s32[]{:S(2)}) async-start(), calls=%async_computation.2 | async-start | bytes 28352512
  273.6 29.4 %collective-permute-start = (bf16[128,768]{0,1:T(8,128)(2,1)}, bf16[128,768]{0,1:T(8,128)(2,1)}, u32[]{:S(2)}, u32[]{:S(2)}) collective-permute-start(bf16[128,768]{0,1:T(8,128)(2,1)} %copy.93), channel_id=1, source_target_pairs={{0,4},{4,8},{8,12},{12,16},{16,20},{20,24},{24,28},{1,5},{5,9},{9,... | collective-permute-start | bytes 589832 | tf_op jit(solution)/shard_map/while/body/eval_jaxpr/ppermute | solution.py:19
  278.3 24.7 %collective-permute-start.1 = (bf16[128,768]{0,1:T(8,128)(2,1)}, bf16[128,768]{0,1:T(8,128)(2,1)}, u32[]{:S(2)}, u32[]{:S(2)}) collective-permute-start(bf16[128,768]{0,1:T(8,128)(2,1)} %copy.94), channel_id=1, source_target_pairs={{0,4},{4,8},{8,12},{12,16},{16,20},{20,24},{24,28},{1,5},{5,9},{9,... | collective-permute-start | bytes 589832 | tf_op jit(solution)/shard_map/while/body/eval_jaxpr/ppermute | solution.py:19
  288.7 10.5 collective-permute-start.2
  290.0 11.3 collective-permute-start.3
  304.7 24.9 %collective-permute-start = (bf16[128,768]{0,1:T(8,128)(2,1)}, bf16[128,768]{0,1:T(8,128)(2,1)}, u32[]{:S(2)}, u32[]{:S(2)}) collective-permute-start(bf16[128,768]{0,1:T(8,128)(2,1)} %copy.93), channel_id=1, source_target_pairs={{0,4},{4,8},{8,12},{12,16},{16,20},{20,24},{24,28},{1,5},{5,9},{9,... | collective-permute-start | bytes 589832 | tf_op jit(solution)/shard_map/while/body/eval_jaxpr/ppermute | solution.py:19
  308.2 21.4 %collective-permute-start.1 = (bf16[128,768]{0,1:T(8,128)(2,1)}, bf16[128,768]{0,1:T(8,128)(2,1)}, u32[]{:S(2)}, u32[]{:S(2)}) collective-permute-start(bf16[128,768]{0,1:T(8,128)(2,1)} %copy.94), channel_id=1, source_target_pairs={{0,4},{4,8},{8,12},{12,16},{16,20},{20,24},{24,28},{1,5},{5,9},{9,... | collective-permute-start | bytes 589832 | tf_op jit(solution)/shard_map/while/body/eval_jaxpr/ppermute | solution.py:19
  316.5 9.3 collective-permute-start.2
  317.8 10.1 collective-permute-start.3
  331.2 24.7 %collective-permute-start = (bf16[128,768]{0,1:T(8,128)(2,1)}, bf16[128,768]{0,1:T(8,128)(2,1)}, u32[]{:S(2)}, u32[]{:S(2)}) collective-permute-start(bf16[128,768]{0,1:T(8,128)(2,1)} %copy.93), channel_id=1, source_target_pairs={{0,4},{4,8},{8,12},{12,16},{16,20},{20,24},{24,28},{1,5},{5,9},{9,... | collective-permute-start | bytes 589832 | tf_op jit(solution)/shard_map/while/body/eval_jaxpr/ppermute | solution.py:19
  334.8 21.1 %collective-permute-start.1 = (bf16[128,768]{0,1:T(8,128)(2,1)}, bf16[128,768]{0,1:T(8,128)(2,1)}, u32[]{:S(2)}, u32[]{:S(2)}) collective-permute-start(bf16[128,768]{0,1:T(8,128)(2,1)} %copy.94), channel_id=1, source_target_pairs={{0,4},{4,8},{8,12},{12,16},{16,20},{20,24},{24,28},{1,5},{5,9},{9,... | collective-permute-start | bytes 589832 | tf_op jit(solution)/shard_map/while/body/eval_jaxpr/ppermute | solution.py:19
  343.4 8.7 collective-permute-start.2
  344.8 9.5 collective-permute-start.3
  357.6 23.7 %collective-permute-start = (bf16[128,768]{0,1:T(8,128)(2,1)}, bf16[128,768]{0,1:T(8,128)(2,1)}, u32[]{:S(2)}, u32[]{:S(2)}) collective-permute-start(bf16[128,768]{0,1:T(8,128)(2,1)} %copy.93), channel_id=1, source_target_pairs={{0,4},{4,8},{8,12},{12,16},{16,20},{20,24},{24,28},{1,5},{5,9},{9,... | collective-permute-start | bytes 589832 | tf_op jit(solution)/shard_map/while/body/eval_jaxpr/ppermute | solution.py:19
  361.1 20.1 %collective-permute-start.1 = (bf16[128,768]{0,1:T(8,128)(2,1)}, bf16[128,768]{0,1:T(8,128)(2,1)}, u32[]{:S(2)}, u32[]{:S(2)}) collective-permute-start(bf16[128,768]{0,1:T(8,128)(2,1)} %copy.94), channel_id=1, source_target_pairs={{0,4},{4,8},{8,12},{12,16},{16,20},{20,24},{24,28},{1,5},{5,9},{9,... | collective-permute-start | bytes 589832 | tf_op jit(solution)/shard_map/while/body/eval_jaxpr/ppermute | solution.py:19
  368.7 8.7 collective-permute-start.2
  370.1 9.5 collective-permute-start.3
  382.9 25.3 %collective-permute-start = (bf16[128,768]{0,1:T(8,128)(2,1)}, bf16[128,768]{0,1:T(8,128)(2,1)}, u32[]{:S(2)}, u32[]{:S(2)}) collective-permute-start(bf16[128,768]{0,1:T(8,128)(2,1)} %copy.93), channel_id=1, source_target_pairs={{0,4},{4,8},{8,12},{12,16},{16,20},{20,24},{24,28},{1,5},{5,9},{9,... | collective-permute-start | bytes 589832 | tf_op jit(solution)/shard_map/while/body/eval_jaxpr/ppermute | solution.py:19
  386.5 21.7 %collective-permute-start.1 = (bf16[128,768]{0,1:T(8,128)(2,1)}, bf16[128,768]{0,1:T(8,128)(2,1)}, u32[]{:S(2)}, u32[]{:S(2)}) collective-permute-start(bf16[128,768]{0,1:T(8,128)(2,1)} %copy.94), channel_id=1, source_target_pairs={{0,4},{4,8},{8,12},{12,16},{16,20},{20,24},{24,28},{1,5},{5,9},{9,... | collective-permute-start | bytes 589832 | tf_op jit(solution)/shard_map/while/body/eval_jaxpr/ppermute | solution.py:19
  397.0 9.5 collective-permute-start.3
  409.8 25.3 %collective-permute-start = (bf16[128,768]{0,1:T(8,128)(2,1)}, bf16[128,768]{0,1:T(8,128)(2,1)}, u32[]{:S(2)}, u32[]{:S(2)}) collective-permute-start(bf16[128,768]{0,1:T(8,128)(2,1)} %copy.93), channel_id=1, source_target_pairs={{0,4},{4,8},{8,12},{12,16},{16,20},{20,24},{24,28},{1,5},{5,9},{9,... | collective-permute-start | bytes 589832 | tf_op jit(solution)/shard_map/while/body/eval_jaxpr/ppermute | solution.py:19
  413.4 21.7 %collective-permute-start.1 = (bf16[128,768]{0,1:T(8,128)(2,1)}, bf16[128,768]{0,1:T(8,128)(2,1)}, u32[]{:S(2)}, u32[]{:S(2)}) collective-permute-start(bf16[128,768]{0,1:T(8,128)(2,1)} %copy.94), channel_id=1, source_target_pairs={{0,4},{4,8},{8,12},{12,16},{16,20},{20,24},{24,28},{1,5},{5,9},{9,... | collective-permute-start | bytes 589832 | tf_op jit(solution)/shard_map/while/body/eval_jaxpr/ppermute | solution.py:19
  422.6 8.7 collective-permute-start.2
  423.9 9.5 collective-permute-start.3
  436.7 23.7 %collective-permute-start = (bf16[128,768]{0,1:T(8,128)(2,1)}, bf16[128,768]{0,1:T(8,128)(2,1)}, u32[]{:S(2)}, u32[]{:S(2)}) collective-permute-start(bf16[128,768]{0,1:T(8,128)(2,1)} %copy.93), channel_id=1, source_target_pairs={{0,4},{4,8},{8,12},{12,16},{16,20},{20,24},{24,28},{1,5},{5,9},{9,... | collective-permute-start | bytes 589832 | tf_op jit(solution)/shard_map/while/body/eval_jaxpr/ppermute | solution.py:19
  440.3 20.1 %collective-permute-start.1 = (bf16[128,768]{0,1:T(8,128)(2,1)}, bf16[128,768]{0,1:T(8,128)(2,1)}, u32[]{:S(2)}, u32[]{:S(2)}) collective-permute-start(bf16[128,768]{0,1:T(8,128)(2,1)} %copy.94), channel_id=1, source_target_pairs={{0,4},{4,8},{8,12},{12,16},{16,20},{20,24},{24,28},{1,5},{5,9},{9,... | collective-permute-start | bytes 589832 | tf_op jit(solution)/shard_map/while/body/eval_jaxpr/ppermute | solution.py:19
  449.2 9.5 collective-permute-start.3
  462.0 25.3 %collective-permute-start = (bf16[128,768]{0,1:T(8,128)(2,1)}, bf16[128,768]{0,1:T(8,128)(2,1)}, u32[]{:S(2)}, u32[]{:S(2)}) collective-permute-start(bf16[128,768]{0,1:T(8,128)(2,1)} %copy.93), channel_id=1, source_target_pairs={{0,4},{4,8},{8,12},{12,16},{16,20},{20,24},{24,28},{1,5},{5,9},{9,... | collective-permute-start | bytes 589832 | tf_op jit(solution)/shard_map/while/body/eval_jaxpr/ppermute | solution.py:19
  465.6 21.7 %collective-permute-start.1 = (bf16[128,768]{0,1:T(8,128)(2,1)}, bf16[128,768]{0,1:T(8,128)(2,1)}, u32[]{:S(2)}, u32[]{:S(2)}) collective-permute-start(bf16[128,768]{0,1:T(8,128)(2,1)} %copy.94), channel_id=1, source_target_pairs={{0,4},{4,8},{8,12},{12,16},{16,20},{20,24},{24,28},{1,5},{5,9},{9,... | collective-permute-start | bytes 589832 | tf_op jit(solution)/shard_map/while/body/eval_jaxpr/ppermute | solution.py:19
  476.1 9.5 collective-permute-start.3
  (120 other events, 625.7 us)
Sparse Core Ops, SparseCore 0:
  12.8 46.6 all-gather.2
  62.2 42.9 all-gather.4
  1120.4 247.8 all-reduce.4
where the time goes:
time: 1440 us; the launch traced here: 1430 us
  blocking collectives  458 us (32%)
  waiting for transfers between devices  358 us (25%)
  local copies, waits for them, and re-layouts  299 us (21%)
  matrix products  131 us (9%)
  other arithmetic  106 us (7%)
  starting transfers between devices  58.3 us (4%)
    unnamed x1, blocking collectives  458 us
    unnamed x4, waiting for transfers between devices  243 us
    unnamed x123, local copies, waits for them, and re-layouts  133 us
    all_gather x1, waiting for transfers between devices, per_device(): v_all = lax.all_gather(v_flat, 'seq', axis=0, tiled=True)  45.8 us
    ppermute x16, starting transfers between devices, from_behind(): return lax.ppermute(shard, axis, pairs)  41.9 us
    all_gather x1, waiting for transfers between devices, per_device(): k_all = lax.all_gather(k_flat, 'seq', axis=0, tiled=True)  38.8 us
    slice x8, local copies, waits for them, and re-layouts, per_device(): outputs.append(whole[offset:offset + extent].reshape(member.shape))  35.9 us
    dot_general x16, matrix products, scores_of(): jnp.einsum('qhd,khd->hqk', q_heads, k_heads, preferred_element_type=jnp.f...  33.6 us
  transfers between devices with their start and end apart: 35, of which 19 were waited for; matrix products, arithmetic and copies ran while one was open for 9% of the time, Pallas kernels for 0%

commit v1 on v0

--- a/solution.py
+++ b/solution.py
@@ -1,8 +1,11 @@
+import functools
 import math
 
 import jax
 import jax.numpy as jnp
 from jax import lax
+from jax.experimental import pallas as pl
+from jax.experimental.pallas import tpu as pltpu
 from jax.sharding import PartitionSpec as P
 
 HEADS = 12
@@ -11,6 +14,228 @@
 
 norm_eps = 1e-05
 masked_low = -1e30
+
+
+MESH_ID = pl.DeviceIdType.MESH
+TILE = 16
+
+
+def running_sum(lengths):
+    places = jnp.arange(lengths.shape[0], dtype=jnp.int32)
+    return jnp.sum(jnp.where(places[None, :] <= places[:, None], lengths[None, :], 0), axis=1)
+
+
+class Place:
+    def __init__(self):
+        self.seq = lax.axis_index("seq")
+        self.batch = lax.axis_index("batch")
+
+    def bit(self, axis):
+        name, k = axis
+        return ((self.seq if name == "seq" else self.batch) // (1 << k)) % 2
+
+    def partner(self, axis):
+        name, k = axis
+        step = (1 << k) * (1 - 2 * self.bit(axis))
+        if name == "seq":
+            return (self.seq + step, self.batch)
+        return (self.seq, self.batch + step)
+
+
+CORE = ("batch", 0)
+ACROSS = ("batch", 1)
+
+
+def seq_axes(peers):
+    return [("seq", k) for k in range((peers - 1).bit_length())]
+
+
+def axis_orders(peers):
+    bits = seq_axes(peers)
+    return [[bits[0], ACROSS] + bits[1:], [ACROSS] + bits, bits[1:] + [bits[0], ACROSS]]
+
+
+def parts_of(rows, stages):
+    found = []
+    for _ in range(stages):
+        halve = (rows // 2) % TILE == 0
+        rows = rows // 2 if halve else rows
+        found.append((rows, halve))
+    return found
+
+
+class Sems:
+    def __init__(self, send, recv):
+        self.send, self.recv, self.count = send, recv, 0
+
+    def take(self):
+        k = self.count
+        self.count += 1
+        return self.send.at[k], self.recv.at[k]
+
+
+def rows_at(start, size):
+    return pl.ds(pl.multiple_of(start, TILE), size)
+
+
+def add_rows(into, one, at, other, other_at, rows):
+    step = 32 if rows % 32 == 0 else TILE
+
+    def body(i, carry):
+        here = rows_at(at + i * step, step)
+        there = rows_at(other_at + i * step, step)
+        both = one[here].astype(jnp.float32) + other[there].astype(jnp.float32)
+        into[here] = both.astype(into.dtype)
+        return carry
+
+    lax.fori_loop(0, rows // step, body, 0)
+
+
+def sum_item(place, sems, buf, at, rows, order, inbox, used, total):
+    low, plan = at, []
+    for k, (axis, (part, halve)) in enumerate(zip(order, parts_of(rows, len(order)))):
+        bit = place.bit(axis)
+        keep, give = (low + bit * part, low + (1 - bit) * part) if halve else (low, low)
+        copy = pltpu.make_async_remote_copy(
+            buf.at[rows_at(give, part)],
+            inbox.at[rows_at(used, part)],
+            *sems.take(),
+            device_id=place.partner(axis),
+            device_id_type=MESH_ID,
+        )
+        copy.start()
+        yield
+        copy.wait()
+        add_rows(total if k == len(order) - 1 else buf, buf, keep, inbox, used, part)
+        plan.append((axis, keep, part, halve))
+        used += part
+        low = keep
+    for axis, keep, part, halve in reversed(plan):
+        if halve:
+            here = rows_at(keep, part)
+            copy = pltpu.make_async_remote_copy(
+                total.at[here],
+                total.at[here],
+                *sems.take(),
+                device_id=place.partner(axis),
+                device_id_type=MESH_ID,
+            )
+            copy.start()
+            yield
+            copy.wait()
+
+
+def take_turns(tasks, enter):
+    live, waiting = [], list(tasks)
+    while live or waiting:
+        live, waiting = live + waiting[:enter], waiting[enter:]
+        still = []
+        for task in live:
+            try:
+                next(task)
+                still.append(task)
+            except StopIteration:
+                pass
+        live = still
+
+
+def sum_kernel(items, orders, small_axes, grads, small, out, small_out, buf, inbox, near, small_in, ssem, rsem, lsem):
+    place = Place()
+    sems = Sems(ssem, rsem)
+    barrier = pltpu.get_barrier_semaphore()
+    for axis in small_axes:
+        pl.semaphore_signal(barrier, inc=1, device_id=place.partner(axis), device_id_type=MESH_ID)
+    pl.semaphore_wait(barrier, len(small_axes))
+    half = buf.shape[0]
+    core = place.bit(CORE)
+    small_out[...] = small[...]
+
+    def small_task():
+        for k, axis in enumerate(small_axes):
+            copy = pltpu.make_async_remote_copy(
+                small_out,
+                small_in.at[k],
+                *sems.take(),
+                device_id=place.partner(axis),
+                device_id_type=MESH_ID,
+            )
+            copy.start()
+            yield
+            copy.wait()
+            small_out[...] += small_in[k]
+
+    def item_task(k, at, rows, order, used):
+        mine = pltpu.make_async_copy(
+            grads.at[rows_at(core * half + at, rows)], buf.at[rows_at(at, rows)], lsem.at[2 * k]
+        )
+        other = pltpu.make_async_remote_copy(
+            grads.at[rows_at((1 - core) * half + at, rows)],
+            near.at[rows_at(at, rows)],
+            *sems.take(),
+            device_id=place.partner(CORE),
+            device_id_type=MESH_ID,
+        )
+        mine.start()
+        other.start()
+        yield
+        mine.wait()
+        other.wait()
+        add_rows(buf, buf, at, near, at, rows)
+        yield from sum_item(place, sems, buf, at, rows, order, inbox, used, near)
+        there = out.at[rows_at(core * half + at, rows)]
+        keep = pltpu.make_async_copy(near.at[rows_at(at, rows)], there, lsem.at[2 * k + 1])
+        give = pltpu.make_async_remote_copy(
+            near.at[rows_at(at, rows)],
+            there,
+            *sems.take(),
+            device_id=place.partner(CORE),
+            device_id_type=MESH_ID,
+        )
+        keep.start()
+        give.start()
+        yield
+        keep.wait()
+        give.wait()
+
+    tasks, at, used = [], 0, 0
+    for k, (rows, kind) in enumerate(items):
+        tasks.append(item_task(k, at, rows, orders[kind], used))
+        at += rows
+        used += sum(part for part, _ in parts_of(rows, len(orders[kind])))
+    take_turns(tasks[:3] + [small_task()] + tasks[3:], 3)
+
+
+def sum_over_devices(grads, small, peers):
+    half = grads.shape[0] // 2
+    width = grads.shape[1]
+    orders = axis_orders(peers)
+    small_axes = [CORE, ACROSS] + seq_axes(peers)
+    unit = 256
+    items = [(unit, k % 3) for k in range(half // unit)]
+    counts = [parts_of(rows, len(orders[kind])) for rows, kind in items]
+    used = sum(part for count in counts for part, _ in count)
+    copies = sum(3 + 2 * len(count) for count in counts) + len(small_axes)
+    return pl.pallas_call(
+        functools.partial(sum_kernel, items, orders, small_axes),
+        out_shape=(
+            jax.ShapeDtypeStruct(grads.shape, jnp.bfloat16),
+            jax.ShapeDtypeStruct(small.shape, jnp.float32),
+        ),
+        in_specs=[pl.BlockSpec(memory_space=pl.ANY), pl.BlockSpec(memory_space=pltpu.VMEM)],
+        out_specs=(pl.BlockSpec(memory_space=pl.ANY), pl.BlockSpec(memory_space=pltpu.VMEM)),
+        scratch_shapes=[
+            pltpu.VMEM((half, width), jnp.bfloat16),
+            pltpu.VMEM((used, width), jnp.bfloat16),
+            pltpu.VMEM((half, width), jnp.bfloat16),
+            pltpu.VMEM((len(small_axes),) + small.shape, jnp.float32),
+            pltpu.SemaphoreType.DMA((copies,)),
+            pltpu.SemaphoreType.DMA((copies,)),
+            pltpu.SemaphoreType.DMA((2 * len(items),)),
+        ],
+        compiler_params=pltpu.CompilerParams(
+            collective_id=1, has_side_effects=True, vmem_limit_bytes=56 * 2**20
+        ),
+    )(grads, small)
 
 
 def from_behind(shard, axis, by):
@@ -105,7 +330,7 @@
     width = inputs.shape[2]
     index = lax.axis_index("seq")
     count = lax.axis_size("seq")
-    ends = jnp.cumsum(doc_lengths[0])
+    ends = running_sum(doc_lengths[0])
     q_place = index * rows + jnp.arange(rows, dtype=jnp.int32)
     q_doc = doc_of(ends, index * rows, rows)
 
@@ -239,16 +464,36 @@
         grad_down_weight,
         grad_down_bias,
     )
-    joined = jnp.concatenate([member.reshape(-1) for member in members])
-    summed = lax.psum_scatter(joined, ("seq", "batch"), scatter_dimension=0, tiled=True)
-    whole = lax.all_gather(
-        summed.astype(jnp.bfloat16), ("seq", "batch"), axis=0, tiled=True
-    ).astype(summed.dtype)
-    outputs = []
+    large = [2, 4, 8, 10]
+    blocks = []
+    for k in large:
+        member = members[k].astype(jnp.bfloat16)
+        for r in range(member.shape[0] // width):
+            for c in range(member.shape[1] // width):
+                blocks.append(member[r * width : (r + 1) * width, c * width : (c + 1) * width])
+    stacked = jnp.stack(blocks).reshape(len(blocks), 2, width // 2, width)
+    grads = jnp.transpose(stacked, (1, 0, 2, 3)).reshape(-1, width)
+    rest = [k for k in range(len(members)) if k not in large]
+    flat = jnp.concatenate([members[k] for k in rest])
+    small_rows = -(-flat.size // (8 * width)) * 8
+    small = jnp.pad(flat, (0, small_rows * width - flat.size)).reshape(small_rows, width)
+    grads, small = sum_over_devices(grads, small, count)
+    flat = small.reshape(-1)
+    blocks = jnp.transpose(grads.reshape(2, len(blocks), width // 2, width), (1, 0, 2, 3))
+    blocks = blocks.reshape(-1, width, width)
+    outputs = [None] * len(members)
+    at = 0
+    for k in large:
+        tall, wide = (extent // width for extent in members[k].shape)
+        rows_of = []
+        for r in range(tall):
+            rows_of.append(jnp.concatenate([blocks[at + r * wide + c] for c in range(wide)], axis=1))
+        outputs[k] = jnp.concatenate(rows_of, axis=0).astype(jnp.float32)
+        at += tall * wide
     offset = 0
-    for member in members:
-        extent = member.size
-        outputs.append(whole[offset : offset + extent].reshape(member.shape))
+    for k in rest:
+        extent = members[k].size
+        outputs[k] = flat[offset : offset + extent]
         offset = offset + extent
     return (
         layer_out,

time: 1440 us -> 706 us (0.49)
  blocking collectives: 458 us -> 0 us
  waiting for transfers between devices: 358 us -> 116 us
  local copies, waits for them, and re-layouts: 299 us -> 133 us
  Pallas kernels: 0 us -> 136 us
  matrix products: 131 us -> 116 us
    unnamed x1 -> x0, blocking collectives: 458 us -> none
    unnamed x4 -> x2, waiting for transfers between devices: 243 us -> 0.71 us
    pallas_call x0 -> x1, Pallas kernels: none -> 136 us  [sum_over_devices(): pl.pallas_call(functools.partial(sum_kernel, items, orders, small_axes),...]
    unnamed x123 -> x144, local copies, waits for them, and re-layouts: 133 us -> 21.1 us
    reshape x5 -> x1, local copies, waits for them, and re-layouts: 40.2 us -> 1.42 us  [per_device(): jnp.pad(flat, (0, small_rows * width - flat.size))]
    convert_element_type x0 -> x4, other arithmetic: none -> 16.3 us  [per_device(): outputs[k] = jnp.concatenate(rows_of, axis=0).astype(jnp.float32)]
    slice x8 -> x9, local copies, waits for them, and re-layouts: 35.9 us -> 20.3 us  [the longest x1 9.34 us: per_device(): blocks[at + r * wide + c]]
  transfers between devices with their start and end apart: 35 -> 34, of which waited for: 19 -> 18; matrix products, arithmetic and copies ran while one was open for 9% -> 17% of each run, Pallas kernels for 0% -> 0%
where the time goes in v1:
time: 706 us; the launch traced here: 700 us
  Pallas kernels  136 us (19%)
  local copies, waits for them, and re-layouts  133 us (19%)
  other arithmetic  119 us (17%)
  matrix products  116 us (16%)
  waiting for transfers between devices  116 us (16%)
  starting transfers between devices  58.2 us (8%)
  between operations  14.8 us (2%)
    pallas_call x1, Pallas kernels, sum_over_devices(): pl.pallas_call(functools.partial(sum_kernel, items, orders, small_axes),...  136 us
    all_gather x1, waiting for transfers between devices, per_device(): v_all = lax.all_gather(v_flat, 'seq', axis=0, tiled=True)  45.8 us
    ppermute x16, starting transfers between devices, from_behind(): return lax.ppermute(shard, axis, pairs)  41.8 us
    all_gather x1, waiting for transfers between devices, per_device(): k_all = lax.all_gather(k_flat, 'seq', axis=0, tiled=True)  39.2 us
    dot_general x16, matrix products, scores_of(): jnp.einsum('qhd,khd->hqk', q_heads, k_heads, preferred_element_type=jnp.f...  33.6 us
    while x152, local copies, waits for them, and re-layouts  31.6 us
    ppermute x16, waiting for transfers between devices, shifted(): return lax.ppermute(block, axis, route)  29.9 us
    dynamic_slice x16, local copies, waits for them, and re-layouts, one(): v_blk = lax.dynamic_slice_in_dim(v_all, offset, rows, 0)  28.3 us
  transfers between devices with their start and end apart: 34, of which 18 were waited for; matrix products, arithmetic and copies ran while one was open for 17% of the time, Pallas kernels for 0%

profile of v1, /device:TPU:0, one launch (start us, length us, event | category | flops | bytes accessed | tf_op | source)
XLA Modules:
  0.0 700.3 jit_solution(11451677569717386250)
XLA Ops:
  20.6 39.2 %all-gather.3.cloned.1.call-done = bf16[1024,768]{1,0:T(8,128)(2,1)} async-done(((bf16[128,768]{1,0:T(8,128)(2,1)}), bf16[1024,768]{1,0:T(8,128)(2,1)}) %all-gather.3.cloned.1.call-update) | async-done | bytes 1572880 | tf_op jit(solution)/shard_map/all_gather | solution.py:361
  59.8 45.8 %all-gather.5.cloned.1.call-done = bf16[1024,768]{1,0:T(8,128)(2,1)} async-done(((bf16[128,768]{1,0:T(8,128)(2,1)}), bf16[1024,768]{1,0:T(8,128)(2,1)}) %all-gather.5.cloned.1.call-update) | async-done | bytes 1572880 | tf_op jit(solution)/shard_map/all_gather | solution.py:362
  106.1 144.1 %while.39 = (s32[]{:T(128)}, f32[12,128]{1,0:T(8,128)}, f32[12,128]{1,0:T(8,128)}, f32[12,128,64]{1,2,0:T(8,128)}, s32[128]{0:T(128)}, /*index=5*/s32[9]{0:T(128...) while((s32[]{:T(128)}, f32[12,128]{1,0:T(8,128)}, ...), condition=%wide.region_8.9_spmd.clone, body=%wide.region_4.8_spmd.clone.sunk | while | flops 54422532 | bytes 5542183 | solution.py:373
  113.0 2.9 select_reduce_fusion.3
  130.3 2.9 select_reduce_fusion.3
  148.4 2.9 select_reduce_fusion.3
  166.5 2.9 select_reduce_fusion.3
  184.6 2.9 select_reduce_fusion.3
  202.7 2.9 select_reduce_fusion.3
  220.9 2.9 select_reduce_fusion.3
  239.0 2.9 select_reduce_fusion.3
  254.0 3.3 convolution_add_fusion.2
  257.4 5.5 convert_reduce_fusion.2
  272.4 215.5 %while.40 = (s32[]{:T(128)}, bf16[128,768]{0,1:T(8,128)(2,1)}, bf16[128,768]{0,1:T(8,128)(2,1)}, f32[128,768]{0,1:T(8,128)}, f32[128,768]{0,1:T(8,128)}, /*index...) while((s32[]{:T(128)}, bf16[128,768]{0,1:T(8,128)(2,1)}, ...), condition=%wide.region_15.16_spmd.clone, body=%wide.region_13.15_spmd.clone.sunk | while | flops 130993680 | bytes 19995340 | solution.py:436
  274.0 3.1 collective-permute-start
  278.8 4.7 collective-permute-start.1
  294.2 5.5 collective-permute-done.2
  322.4 3.9 collective-permute-done.2
  335.3 3.0 collective-permute-start.1
  348.1 4.5 collective-permute-done.2
  387.0 3.6 collective-permute-start.1
  397.5 2.8 collective-permute-start.3
  413.9 3.6 collective-permute-start.1
  428.0 3.8 collective-permute-done.2
  466.2 3.5 collective-permute-start.1
  476.7 2.8 collective-permute-start.3
  524.0 136.3 %shard_map.254 = (bf16[9216,768]{1,0:T(8,128)(2,1)}, f32[16,768]{1,0:T(8,128)}) custom-call(bf16[9216,768]{1,0:T(8,128)(2,1)} %bitcast.214, f32[16,768]{1,0:T(8,128)} %reshape.367.small), custom_call_target="tpu_custom_call" | custom-call | tf_op jit(solution)/shard_map/pallas_call | solution.py:218
  665.9 9.3 %fusion.66 = (bf16[1,2,384,768]{3,2,0,1:T(8,128)(2,1)}, bf16[1,2,384,768]{3,2,0,1:T(8,128)(2,1)}, bf16[1,2,384,768]{3,2,0,1:T(8,128)(2,1)}, bf16[1,2,384,768]{3,...) fusion(bf16[12,2,384,768]{3,2,0,1:T(8,128)(2,1)} %bitcast.215), kind=kLoop, calls=%fused_computation.158 | loop fusion | bytes 28311552 | tf_op jit(solution)/shard_map/slice | solution.py:490
  676.5 2.8 bitcast_convert_fusion
  680.0 4.7 maximum_convert_fusion.2
  684.7 4.5 maximum_convert_fusion
  689.3 4.2 maximum_convert_fusion.1
  (604 shorter events, 355.6 us)
Async XLA Ops:
  7.2 52.6 %all-gather.3.cloned.1.call-start = ((), (), s32[]{:S(2)}) async-start(), calls=%async_computation | async-start | bytes 1769472 | tf_op jit(solution)/shard_map/all_gather | solution.py:361
  12.7 92.9 %all-gather.5.cloned.1.call-start = ((), (), s32[]{:S(2)}) async-start(), calls=%async_computation.1 | async-start | bytes 1769472 | tf_op jit(solution)/shard_map/all_gather | solution.py:362
  274.0 29.5 %collective-permute-start = (bf16[128,768]{0,1:T(8,128)(2,1)}, bf16[128,768]{0,1:T(8,128)(2,1)}, u32[]{:S(2)}, u32[]{:S(2)}) collective-permute-start(bf16[128,768]{0,1:T(8,128)(2,1)} %copy.121), channel_id=1, source_target_pairs={{0,4},{4,8},{8,12},{12,16},{16,20},{20,24},{24,28},{1,5},{5,9},{9,... | collective-permute-start | bytes 589832 | tf_op jit(solution)/shard_map/while/body/eval_jaxpr/ppermute | solution.py:244
  278.8 24.7 %collective-permute-start.1 = (bf16[128,768]{0,1:T(8,128)(2,1)}, bf16[128,768]{0,1:T(8,128)(2,1)}, u32[]{:S(2)}, u32[]{:S(2)}) collective-permute-start(bf16[128,768]{0,1:T(8,128)(2,1)} %copy.122), channel_id=1, source_target_pairs={{0,4},{4,8},{8,12},{12,16},{16,20},{20,24},{24,28},{1,5},{5,9},{9,... | collective-permute-start | bytes 589832 | tf_op jit(solution)/shard_map/while/body/eval_jaxpr/ppermute | solution.py:244
  289.1 10.5 %collective-permute-start.2 = (bf16[128,768]{0,1:T(8,128)(2,1)}, bf16[128,768]{0,1:T(8,128)(2,1)}, u32[]{:S(2)}, u32[]{:S(2)}) collective-permute-start(bf16[128,768]{0,1:T(8,128)(2,1)} %fusion.137), channel_id=1, source_target_pairs={{28,0},{0,4},{4,8},{8,12},{12,16},{16,20},{20,24},{24,28},{29,1},{... | collective-permute-start | bytes 589832 | tf_op jit(solution)/shard_map/while/body/eval_jaxpr/ppermute | solution.py:250
  290.4 11.3 %collective-permute-start.3 = (bf16[128,768]{0,1:T(8,128)(2,1)}, bf16[128,768]{0,1:T(8,128)(2,1)}, u32[]{:S(2)}, u32[]{:S(2)}) collective-permute-start(bf16[128,768]{0,1:T(8,128)(2,1)} %fusion.139), channel_id=1, source_target_pairs={{28,0},{0,4},{4,8},{8,12},{12,16},{16,20},{20,24},{24,28},{29,1},{... | collective-permute-start | bytes 589832 | tf_op jit(solution)/shard_map/while/body/eval_jaxpr/ppermute | solution.py:250
  305.1 25.0 %collective-permute-start = (bf16[128,768]{0,1:T(8,128)(2,1)}, bf16[128,768]{0,1:T(8,128)(2,1)}, u32[]{:S(2)}, u32[]{:S(2)}) collective-permute-start(bf16[128,768]{0,1:T(8,128)(2,1)} %copy.121), channel_id=1, source_target_pairs={{0,4},{4,8},{8,12},{12,16},{16,20},{20,24},{24,28},{1,5},{5,9},{9,... | collective-permute-start | bytes 589832 | tf_op jit(solution)/shard_map/while/body/eval_jaxpr/ppermute | solution.py:244
  308.7 21.4 %collective-permute-start.1 = (bf16[128,768]{0,1:T(8,128)(2,1)}, bf16[128,768]{0,1:T(8,128)(2,1)}, u32[]{:S(2)}, u32[]{:S(2)}) collective-permute-start(bf16[128,768]{0,1:T(8,128)(2,1)} %copy.122), channel_id=1, source_target_pairs={{0,4},{4,8},{8,12},{12,16},{16,20},{20,24},{24,28},{1,5},{5,9},{9,... | collective-permute-start | bytes 589832 | tf_op jit(solution)/shard_map/while/body/eval_jaxpr/ppermute | solution.py:244
  317.0 9.3 %collective-permute-start.2 = (bf16[128,768]{0,1:T(8,128)(2,1)}, bf16[128,768]{0,1:T(8,128)(2,1)}, u32[]{:S(2)}, u32[]{:S(2)}) collective-permute-start(bf16[128,768]{0,1:T(8,128)(2,1)} %fusion.137), channel_id=1, source_target_pairs={{28,0},{0,4},{4,8},{8,12},{12,16},{16,20},{20,24},{24,28},{29,1},{... | collective-permute-start | bytes 589832 | tf_op jit(solution)/shard_map/while/body/eval_jaxpr/ppermute | solution.py:250
  318.3 10.1 %collective-permute-start.3 = (bf16[128,768]{0,1:T(8,128)(2,1)}, bf16[128,768]{0,1:T(8,128)(2,1)}, u32[]{:S(2)}, u32[]{:S(2)}) collective-permute-start(bf16[128,768]{0,1:T(8,128)(2,1)} %fusion.139), channel_id=1, source_target_pairs={{28,0},{0,4},{4,8},{8,12},{12,16},{16,20},{20,24},{24,28},{29,1},{... | collective-permute-start | bytes 589832 | tf_op jit(solution)/shard_map/while/body/eval_jaxpr/ppermute | solution.py:250
  331.7 24.7 %collective-permute-start = (bf16[128,768]{0,1:T(8,128)(2,1)}, bf16[128,768]{0,1:T(8,128)(2,1)}, u32[]{:S(2)}, u32[]{:S(2)}) collective-permute-start(bf16[128,768]{0,1:T(8,128)(2,1)} %copy.121), channel_id=1, source_target_pairs={{0,4},{4,8},{8,12},{12,16},{16,20},{20,24},{24,28},{1,5},{5,9},{9,... | collective-permute-start | bytes 589832 | tf_op jit(solution)/shard_map/while/body/eval_jaxpr/ppermute | solution.py:244
  335.3 21.1 %collective-permute-start.1 = (bf16[128,768]{0,1:T(8,128)(2,1)}, bf16[128,768]{0,1:T(8,128)(2,1)}, u32[]{:S(2)}, u32[]{:S(2)}) collective-permute-start(bf16[128,768]{0,1:T(8,128)(2,1)} %copy.122), channel_id=1, source_target_pairs={{0,4},{4,8},{8,12},{12,16},{16,20},{20,24},{24,28},{1,5},{5,9},{9,... | collective-permute-start | bytes 589832 | tf_op jit(solution)/shard_map/while/body/eval_jaxpr/ppermute | solution.py:244
  343.9 8.7 %collective-permute-start.2 = (bf16[128,768]{0,1:T(8,128)(2,1)}, bf16[128,768]{0,1:T(8,128)(2,1)}, u32[]{:S(2)}, u32[]{:S(2)}) collective-permute-start(bf16[128,768]{0,1:T(8,128)(2,1)} %fusion.137), channel_id=1, source_target_pairs={{28,0},{0,4},{4,8},{8,12},{12,16},{16,20},{20,24},{24,28},{29,1},{... | collective-permute-start | bytes 589832 | tf_op jit(solution)/shard_map/while/body/eval_jaxpr/ppermute | solution.py:250
  345.2 9.5 %collective-permute-start.3 = (bf16[128,768]{0,1:T(8,128)(2,1)}, bf16[128,768]{0,1:T(8,128)(2,1)}, u32[]{:S(2)}, u32[]{:S(2)}) collective-permute-start(bf16[128,768]{0,1:T(8,128)(2,1)} %fusion.139), channel_id=1, source_target_pairs={{28,0},{0,4},{4,8},{8,12},{12,16},{16,20},{20,24},{24,28},{29,1},{... | collective-permute-start | bytes 589832 | tf_op jit(solution)/shard_map/while/body/eval_jaxpr/ppermute | solution.py:250
  358.1 23.7 %collective-permute-start = (bf16[128,768]{0,1:T(8,128)(2,1)}, bf16[128,768]{0,1:T(8,128)(2,1)}, u32[]{:S(2)}, u32[]{:S(2)}) collective-permute-start(bf16[128,768]{0,1:T(8,128)(2,1)} %copy.121), channel_id=1, source_target_pairs={{0,4},{4,8},{8,12},{12,16},{16,20},{20,24},{24,28},{1,5},{5,9},{9,... | collective-permute-start | bytes 589832 | tf_op jit(solution)/shard_map/while/body/eval_jaxpr/ppermute | solution.py:244
  361.7 20.1 %collective-permute-start.1 = (bf16[128,768]{0,1:T(8,128)(2,1)}, bf16[128,768]{0,1:T(8,128)(2,1)}, u32[]{:S(2)}, u32[]{:S(2)}) collective-permute-start(bf16[128,768]{0,1:T(8,128)(2,1)} %copy.122), channel_id=1, source_target_pairs={{0,4},{4,8},{8,12},{12,16},{16,20},{20,24},{24,28},{1,5},{5,9},{9,... | collective-permute-start | bytes 589832 | tf_op jit(solution)/shard_map/while/body/eval_jaxpr/ppermute | solution.py:244
  370.6 9.5 %collective-permute-start.3 = (bf16[128,768]{0,1:T(8,128)(2,1)}, bf16[128,768]{0,1:T(8,128)(2,1)}, u32[]{:S(2)}, u32[]{:S(2)}) collective-permute-start(bf16[128,768]{0,1:T(8,128)(2,1)} %fusion.139), channel_id=1, source_target_pairs={{28,0},{0,4},{4,8},{8,12},{12,16},{16,20},{20,24},{24,28},{29,1},{... | collective-permute-start | bytes 589832 | tf_op jit(solution)/shard_map/while/body/eval_jaxpr/ppermute | solution.py:250
  383.4 25.3 %collective-permute-start = (bf16[128,768]{0,1:T(8,128)(2,1)}, bf16[128,768]{0,1:T(8,128)(2,1)}, u32[]{:S(2)}, u32[]{:S(2)}) collective-permute-start(bf16[128,768]{0,1:T(8,128)(2,1)} %copy.121), channel_id=1, source_target_pairs={{0,4},{4,8},{8,12},{12,16},{16,20},{20,24},{24,28},{1,5},{5,9},{9,... | collective-permute-start | bytes 589832 | tf_op jit(solution)/shard_map/while/body/eval_jaxpr/ppermute | solution.py:244
  387.0 21.7 %collective-permute-start.1 = (bf16[128,768]{0,1:T(8,128)(2,1)}, bf16[128,768]{0,1:T(8,128)(2,1)}, u32[]{:S(2)}, u32[]{:S(2)}) collective-permute-start(bf16[128,768]{0,1:T(8,128)(2,1)} %copy.122), channel_id=1, source_target_pairs={{0,4},{4,8},{8,12},{12,16},{16,20},{20,24},{24,28},{1,5},{5,9},{9,... | collective-permute-start | bytes 589832 | tf_op jit(solution)/shard_map/while/body/eval_jaxpr/ppermute | solution.py:244
  396.2 8.7 %collective-permute-start.2 = (bf16[128,768]{0,1:T(8,128)(2,1)}, bf16[128,768]{0,1:T(8,128)(2,1)}, u32[]{:S(2)}, u32[]{:S(2)}) collective-permute-start(bf16[128,768]{0,1:T(8,128)(2,1)} %fusion.137), channel_id=1, source_target_pairs={{28,0},{0,4},{4,8},{8,12},{12,16},{16,20},{20,24},{24,28},{29,1},{... | collective-permute-start | bytes 589832 | tf_op jit(solution)/shard_map/while/body/eval_jaxpr/ppermute | solution.py:250
  397.5 9.5 %collective-permute-start.3 = (bf16[128,768]{0,1:T(8,128)(2,1)}, bf16[128,768]{0,1:T(8,128)(2,1)}, u32[]{:S(2)}, u32[]{:S(2)}) collective-permute-start(bf16[128,768]{0,1:T(8,128)(2,1)} %fusion.139), channel_id=1, source_target_pairs={{28,0},{0,4},{4,8},{8,12},{12,16},{16,20},{20,24},{24,28},{29,1},{... | collective-permute-start | bytes 589832 | tf_op jit(solution)/shard_map/while/body/eval_jaxpr/ppermute | solution.py:250
  410.3 25.3 %collective-permute-start = (bf16[128,768]{0,1:T(8,128)(2,1)}, bf16[128,768]{0,1:T(8,128)(2,1)}, u32[]{:S(2)}, u32[]{:S(2)}) collective-permute-start(bf16[128,768]{0,1:T(8,128)(2,1)} %copy.121), channel_id=1, source_target_pairs={{0,4},{4,8},{8,12},{12,16},{16,20},{20,24},{24,28},{1,5},{5,9},{9,... | collective-permute-start | bytes 589832 | tf_op jit(solution)/shard_map/while/body/eval_jaxpr/ppermute | solution.py:244
  413.9 21.7 %collective-permute-start.1 = (bf16[128,768]{0,1:T(8,128)(2,1)}, bf16[128,768]{0,1:T(8,128)(2,1)}, u32[]{:S(2)}, u32[]{:S(2)}) collective-permute-start(bf16[128,768]{0,1:T(8,128)(2,1)} %copy.122), channel_id=1, source_target_pairs={{0,4},{4,8},{8,12},{12,16},{16,20},{20,24},{24,28},{1,5},{5,9},{9,... | collective-permute-start | bytes 589832 | tf_op jit(solution)/shard_map/while/body/eval_jaxpr/ppermute | solution.py:244
  424.5 9.5 %collective-permute-start.3 = (bf16[128,768]{0,1:T(8,128)(2,1)}, bf16[128,768]{0,1:T(8,128)(2,1)}, u32[]{:S(2)}, u32[]{:S(2)}) collective-permute-start(bf16[128,768]{0,1:T(8,128)(2,1)} %fusion.139), channel_id=1, source_target_pairs={{28,0},{0,4},{4,8},{8,12},{12,16},{16,20},{20,24},{24,28},{29,1},{... | collective-permute-start | bytes 589832 | tf_op jit(solution)/shard_map/while/body/eval_jaxpr/ppermute | solution.py:250
  437.3 23.7 %collective-permute-start = (bf16[128,768]{0,1:T(8,128)(2,1)}, bf16[128,768]{0,1:T(8,128)(2,1)}, u32[]{:S(2)}, u32[]{:S(2)}) collective-permute-start(bf16[128,768]{0,1:T(8,128)(2,1)} %copy.121), channel_id=1, source_target_pairs={{0,4},{4,8},{8,12},{12,16},{16,20},{20,24},{24,28},{1,5},{5,9},{9,... | collective-permute-start | bytes 589832 | tf_op jit(solution)/shard_map/while/body/eval_jaxpr/ppermute | solution.py:244
  440.9 20.1 %collective-permute-start.1 = (bf16[128,768]{0,1:T(8,128)(2,1)}, bf16[128,768]{0,1:T(8,128)(2,1)}, u32[]{:S(2)}, u32[]{:S(2)}) collective-permute-start(bf16[128,768]{0,1:T(8,128)(2,1)} %copy.122), channel_id=1, source_target_pairs={{0,4},{4,8},{8,12},{12,16},{16,20},{20,24},{24,28},{1,5},{5,9},{9,... | collective-permute-start | bytes 589832 | tf_op jit(solution)/shard_map/while/body/eval_jaxpr/ppermute | solution.py:244
  448.5 8.7 %collective-permute-start.2 = (bf16[128,768]{0,1:T(8,128)(2,1)}, bf16[128,768]{0,1:T(8,128)(2,1)}, u32[]{:S(2)}, u32[]{:S(2)}) collective-permute-start(bf16[128,768]{0,1:T(8,128)(2,1)} %fusion.137), channel_id=1, source_target_pairs={{28,0},{0,4},{4,8},{8,12},{12,16},{16,20},{20,24},{24,28},{29,1},{... | collective-permute-start | bytes 589832 | tf_op jit(solution)/shard_map/while/body/eval_jaxpr/ppermute | solution.py:250
  449.8 9.5 %collective-permute-start.3 = (bf16[128,768]{0,1:T(8,128)(2,1)}, bf16[128,768]{0,1:T(8,128)(2,1)}, u32[]{:S(2)}, u32[]{:S(2)}) collective-permute-start(bf16[128,768]{0,1:T(8,128)(2,1)} %fusion.139), channel_id=1, source_target_pairs={{28,0},{0,4},{4,8},{8,12},{12,16},{16,20},{20,24},{24,28},{29,1},{... | collective-permute-start | bytes 589832 | tf_op jit(solution)/shard_map/while/body/eval_jaxpr/ppermute | solution.py:250
  462.7 25.3 %collective-permute-start = (bf16[128,768]{0,1:T(8,128)(2,1)}, bf16[128,768]{0,1:T(8,128)(2,1)}, u32[]{:S(2)}, u32[]{:S(2)}) collective-permute-start(bf16[128,768]{0,1:T(8,128)(2,1)} %copy.121), channel_id=1, source_target_pairs={{0,4},{4,8},{8,12},{12,16},{16,20},{20,24},{24,28},{1,5},{5,9},{9,... | collective-permute-start | bytes 589832 | tf_op jit(solution)/shard_map/while/body/eval_jaxpr/ppermute | solution.py:244
  466.2 21.7 %collective-permute-start.1 = (bf16[128,768]{0,1:T(8,128)(2,1)}, bf16[128,768]{0,1:T(8,128)(2,1)}, u32[]{:S(2)}, u32[]{:S(2)}) collective-permute-start(bf16[128,768]{0,1:T(8,128)(2,1)} %copy.122), channel_id=1, source_target_pairs={{0,4},{4,8},{8,12},{12,16},{16,20},{20,24},{24,28},{1,5},{5,9},{9,... | collective-permute-start | bytes 589832 | tf_op jit(solution)/shard_map/while/body/eval_jaxpr/ppermute | solution.py:244
  475.4 8.7 %collective-permute-start.2 = (bf16[128,768]{0,1:T(8,128)(2,1)}, bf16[128,768]{0,1:T(8,128)(2,1)}, u32[]{:S(2)}, u32[]{:S(2)}) collective-permute-start(bf16[128,768]{0,1:T(8,128)(2,1)} %fusion.137), channel_id=1, source_target_pairs={{28,0},{0,4},{4,8},{8,12},{12,16},{16,20},{20,24},{24,28},{29,1},{... | collective-permute-start | bytes 589832 | tf_op jit(solution)/shard_map/while/body/eval_jaxpr/ppermute | solution.py:250
  476.7 9.5 %collective-permute-start.3 = (bf16[128,768]{0,1:T(8,128)(2,1)}, bf16[128,768]{0,1:T(8,128)(2,1)}, u32[]{:S(2)}, u32[]{:S(2)}) collective-permute-start(bf16[128,768]{0,1:T(8,128)(2,1)} %fusion.139), channel_id=1, source_target_pairs={{28,0},{0,4},{4,8},{8,12},{12,16},{16,20},{20,24},{24,28},{29,1},{... | collective-permute-start | bytes 589832 | tf_op jit(solution)/shard_map/while/body/eval_jaxpr/ppermute | solution.py:250
  (128 other events, 1112.4 us)
Sparse Core Ops, SparseCore 0:
  12.8 46.9 all-gather.2
  62.5 42.9 all-gather.4

commit v2 on v0

v2 whole, which is shorter than its diff:
```python
import functools
import math

import jax
import jax.numpy as jnp
from jax import lax
from jax.experimental import pallas as pl
from jax.experimental.pallas import tpu as pltpu
from jax.sharding import PartitionSpec as P

HEADS = 12
HD = 64


norm_eps = 1e-05
masked_low = -1e30


MESH_ID = pl.DeviceIdType.MESH
TILE = 16
LANES = 128
FF_TILE = 768
ITEM = 256
KINDS = "012"
GROUPS = 5
PACE = 8


def running_sum(lengths):
    places = jnp.arange(lengths.shape[0], dtype=jnp.int32)
    return jnp.sum(jnp.where(places[None, :] <= places[:, None], lengths[None, :], 0), axis=1)


class Place:
    def __init__(self):
        self.seq = lax.axis_index("seq")
        self.batch = lax.axis_index("batch")

    def bit(self, axis):
        name, k = axis
        return ((self.seq if name == "seq" else self.batch) // (1 << k)) % 2

    def partner(self, axis):
        name, k = axis
        step = (1 << k) * (1 - 2 * self.bit(axis))
        if name == "seq":
            return (self.seq + step, self.batch)
        return (self.seq, self.batch + step)


CORE = ("batch", 0)
ACROSS = ("batch", 1)


def seq_axes(peers):
    return [("seq", k) for k in range((peers - 1).bit_length())]


def axis_orders(peers):
    bits = seq_axes(peers)
    return [[bits[0], ACROSS] + bits[1:], [ACROSS] + bits, bits[1:] + [bits[0], ACROSS]]


def parts_of(rows, stages):
    found = []
    for _ in range(stages):
        halve = (rows // 2) % TILE == 0
        rows = rows // 2 if halve else rows
        found.append((rows, halve))
    return found


class Sems:
    def __init__(self, send, recv):
        self.send, self.recv, self.count = send, recv, 0

    def take(self):
        k = self.count
        self.count += 1
        return self.send.at[k], self.recv.at[k]


def rows_at(start, size):
    return pl.ds(pl.multiple_of(start, TILE), size)


def add_rows(into, one, at, other, other_at, rows):
    step = 32 if rows % 32 == 0 else TILE

    def body(i, carry):
        here = rows_at(at + i * step, step)
        there = rows_at(other_at + i * step, step)
        both = one[here].astype(jnp.float32) + other[there].astype(jnp.float32)
        into[here] = both.astype(into.dtype)
        return carry

    lax.fori_loop(0, rows // step, body, 0)


def sum_item(place, sems, buf, at, rows, order, inbox, used, total):
    low, plan = at, []
    for k, (axis, (part, halve)) in enumerate(zip(order, parts_of(rows, len(order)))):
        bit = place.bit(axis)
        keep, give = (low + bit * part, low + (1 - bit) * part) if halve else (low, low)
        copy = pltpu.make_async_remote_copy(
            buf.at[rows_at(give, part)],
            inbox.at[rows_at(used, part)],
            *sems.take(),
            device_id=place.partner(axis),
            device_id_type=MESH_ID,
        )
        copy.start()
        yield
        copy.wait()
        add_rows(total if k == len(order) - 1 else buf, buf, keep, inbox, used, part)
        plan.append((axis, keep, part, halve))
        used += part
        low = keep
    for axis, keep, part, halve in reversed(plan):
        if halve:
            here = rows_at(keep, part)
            copy = pltpu.make_async_remote_copy(
                total.at[here],
                total.at[here],
                *sems.take(),
                device_id=place.partner(axis),
                device_id_type=MESH_ID,
            )
            copy.start()
            yield
            copy.wait()


def dot(a, b, dims=((1,), (0,))):
    return lax.dot_general(a, b, (dims, ((), ())), preferred_element_type=jnp.float32)


NT = ((1,), (1,))
TN = ((0,), (0,))


def norm_parts(rows):
    center = rows - jnp.mean(rows, axis=-1, keepdims=True)
    spread = jnp.mean(center * center, axis=-1, keepdims=True)
    inverse = lax.rsqrt(spread + norm_eps)
    return center * inverse, inverse


def norm_back(grad, unit, inverse, gain):
    scaled = grad * gain
    along = jnp.mean(scaled * unit, axis=-1, keepdims=True)
    return inverse * (scaled - jnp.mean(scaled, axis=-1, keepdims=True) - unit * along)


def doc_ids(ends, places):
    found = jnp.zeros(places.shape, jnp.int32)
    for k in range(ends.shape[0]):
        found += (ends[k] <= places).astype(jnp.int32)
    return found


def places_down(first, rows):
    return first + lax.broadcasted_iota(jnp.int32, (rows, 1), 0)


def places_along(first, rows):
    return first + lax.broadcasted_iota(jnp.int32, (1, rows), 1)


def mask_of(ends, q_places, k_places):
    allowed = (doc_ids(ends, q_places) == doc_ids(ends, k_places)) & (k_places <= q_places)
    return jnp.where(allowed, 0.0, masked_low)


def first_half():
    return lax.broadcasted_iota(jnp.int32, (1, LANES), 1) < HD


def both_heads(pair):
    left = first_half()
    none = jnp.zeros_like(pair)
    return jnp.concatenate([jnp.where(left, pair, none), jnp.where(left, none, pair)], axis=0)


def own_columns(stacked):
    rows = stacked.shape[0] // 2
    return jnp.where(first_half(), stacked[:rows], stacked[rows:])


def lanes(p):
    return pl.ds(p * LANES, LANES)


def forward_kernel(
    nz, n_ends, x_ref, e_ref, ends, gain_one, shift_one, qkv_bias, proj_bias, gain_two, shift_two, up_bias, down_bias,
    qkv_hbm, proj_hbm, up_hbm, down_hbm,
    layer_out, n1_all, q_out, attn_out, da_out, do_out, n2_out, g_out, du_out, dx_out, stats_out, small_out,
    x_all, qkv_w, proj_w, up_w, down_w, kv, mask, top, total, acc, two_q, res_acc, dh_acc,
    up_send, up_recv, down_send, down_recv, side_send, side_recv, w_sem,
):
    rows, width = x_ref.shape
    pair = 2 * rows
    seq = lax.axis_index("seq")
    batch = lax.axis_index("batch")
    z = seq // 2
    x = seq % 2
    loads = [
        pltpu.make_async_copy(hbm, vmem, w_sem.at[k])
        for k, (hbm, vmem) in enumerate(
            [(qkv_hbm, qkv_w), (proj_hbm, proj_w), (up_hbm, up_w), (down_hbm, down_w)]
        )
    ]
    loads[0].start()
    barrier = pltpu.get_barrier_semaphore()
    has_up = z + 1 < nz
    has_down = z > 0
    above = (seq + 2, batch)
    below = (seq - 2, batch)
    beside = (seq + 1 - 2 * x, batch)

    @pl.when(has_up)
    def _():
        pl.semaphore_signal(barrier, inc=1, device_id=above, device_id_type=MESH_ID)

    @pl.when(has_down)
    def _():
        pl.semaphore_signal(barrier, inc=1, device_id=below, device_id_type=MESH_ID)

    pl.semaphore_signal(barrier, inc=1, device_id=beside, device_id_type=MESH_ID)
    pl.semaphore_wait(barrier, 1 + has_up.astype(jnp.int32) + has_down.astype(jnp.int32))
    for load in loads[1:]:
        load.start()

    def block(level, side):
        return x_all.at[rows_at((2 * level + side) * rows, rows)]

    def send(source, level, to, send_sem, recv_sem):
        return pltpu.make_async_remote_copy(
            source, block(level, x), send_sem.at[level], recv_sem.at[level], device_id=to, device_id_type=MESH_ID
        )

    def up_copy(source, level):
        return send(source, level, above, up_send, up_recv)

    def down_copy(source, level):
        return send(source, level, below, down_send, down_recv)

    def side_copy(source, level):
        return send(source, level, beside, side_send, side_recv)

    def wait_side(level):
        pltpu.make_async_remote_copy(
            x_ref, block(level, 1 - x), side_send.at[level], side_recv.at[level], device_id=beside, device_id_type=MESH_ID
        ).wait_recv()

    @pl.when(has_up)
    def _():
        up_copy(x_ref, z).start()

    side_copy(x_ref, z).start()

    @pl.when(has_down)
    def _():
        down_copy(x_ref, z).start()

    x_all[rows_at(seq * rows, rows)] = x_ref[...]
    x32 = x_ref[...].astype(jnp.float32)
    unit_one, _ = norm_parts(x32)
    mine = (unit_one * gain_one[...] + shift_one[...]).astype(jnp.bfloat16)
    top[...] = jnp.full(top.shape, masked_low, jnp.float32)
    total[...] = jnp.zeros(total.shape, jnp.float32)
    acc[...] = jnp.zeros(acc.shape, jnp.float32)
    loads[0].wait()
    q = (dot(mine, qkv_w[:, :width]) + qkv_bias[:, :width]).astype(jnp.bfloat16)
    q = q * jnp.asarray(1.0 / math.sqrt(HD), jnp.bfloat16)
    q_out[...] = q
    for p in range(HEADS // 2):
        two_q[p] = both_heads(q[:, p * LANES : (p + 1) * LANES])

    def pass_on(d):
        @pl.when(z >= d)
        def _():
            level = z - d
            up_copy(x_ref, level).wait_recv()

            @pl.when(has_up)
            def _():
                up_copy(block(level, x), level).start()

            side_copy(block(level, x), level).start()

        @pl.when(z + d < nz)
        def _():
            level = z + d
            down_copy(x_ref, level).wait_recv()

            @pl.when(has_down)
            def _():
                down_copy(block(level, x), level).start()

            side_copy(block(level, x), level).start()

    def normalize(level):
        here = rows_at(level * pair, pair)
        unit, _ = norm_parts(x_all[here].astype(jnp.float32))
        n1 = (unit * gain_one[...] + shift_one[...]).astype(jnp.bfloat16)
        n1_all[here] = n1
        return n1

    def attend(level):
        wait_side(level)
        n1 = normalize(level)
        kv[...] = (dot(n1, qkv_w[:, width:]) + qkv_bias[:, width:]).astype(jnp.bfloat16)
        one = mask_of(ends, places_down(seq * rows, rows), places_along(level * pair, pair))
        mask[:rows] = one
        mask[rows:] = one
        for p in range(HEADS // 2):
            k_pair = kv[:, p * LANES : (p + 1) * LANES]
            v_pair = kv[:, width + p * LANES : width + (p + 1) * LANES]
            s = dot(two_q[p], k_pair, NT)
            low = mask[...]
            before = top[p][:, :1]
            newer = jnp.maximum(before, jnp.max(jnp.abs(s) + low, axis=1, keepdims=True))
            low = low - newer
            plus = jnp.exp(low + s)
            minus = jnp.exp(low - s)
            keep = jnp.exp(before - newer)
            total[p] = total[p] * keep + jnp.sum(plus + minus, axis=1, keepdims=True)
            top[p] = jnp.broadcast_to(newer, (pair, LANES))
            out = own_columns(dot((plus - minus).astype(jnp.bfloat16), v_pair))
            keep = own_columns(jnp.broadcast_to(keep, (pair, LANES)))
            here = slice(p * LANES, (p + 1) * LANES)
            acc[:, here] = acc[:, here] * keep + out

    def level_step(d, carry):
        @pl.when(d + 1 < nz)
        def _():
            pass_on(d + 1)

        @pl.when(z >= d)
        def _():
            attend(z - d)

        @pl.when((d > 0) & (z + d < nz))
        def _():
            wait_side(z + d)
            normalize(z + d)

        return carry

    lax.fori_loop(0, nz, level_step, 0)

    column = lax.broadcasted_iota(jnp.int32, (1, LANES), 1)
    log_total = jnp.zeros((rows, LANES), jnp.float32)
    for p in range(HEADS // 2):
        here = slice(p * LANES, (p + 1) * LANES)
        acc[:, here] = acc[:, here] / own_columns(total[p])
        lse = top[p] + jnp.log(total[p])
        log_total = jnp.where(column == 2 * p, lse[:rows], log_total)
        log_total = jnp.where(column == 2 * p + 1, lse[rows:], log_total)
    attn = acc[...].astype(jnp.bfloat16)
    attn_out[...] = attn
    loads[1].wait()
    resid = x32 + dot(attn, proj_w[...]) + proj_bias[...]
    unit, inverse = norm_parts(resid)
    n2 = (unit * gain_two[...] + shift_two[...]).astype(jnp.bfloat16)
    n2_out[...] = n2
    res_acc[...] = resid + down_bias[...]
    dh_acc[...] = jnp.zeros(dh_acc.shape, jnp.float32)
    loads[2].wait()
    loads[3].wait()
    slope = math.sqrt(2.0 / math.pi)

    def ff_step(t, carry):
        here = pl.ds(pl.multiple_of(t * FF_TILE, FF_TILE), FF_TILE)
        u = dot(n2_out[...], up_w[:, here]) + up_bias[:, here]
        square = u * u
        bend = jnp.tanh(slope * (u + 0.044715 * (square * u)))
        half = 0.5 * (1.0 + bend)
        g = (u * half).astype(jnp.bfloat16)
        slant = half + (0.5 * u) * (1.0 - bend * bend) * (slope * (1.0 + 3.0 * 0.044715 * square))
        g_out[:, here] = g
        res_acc[...] += dot(g, down_w[here])
        du32 = dot(e_ref[...], down_w[here], NT) * slant
        du = du32.astype(jnp.bfloat16)
        du_out[:, here] = du
        small_out[pl.ds(4 + t, 1)] = jnp.sum(du.astype(jnp.float32), axis=0, keepdims=True)
        dh_acc[...] += dot(du, up_w[:, here], NT)
        return carry

    lax.fori_loop(0, up_w.shape[1] // FF_TILE, ff_step, 0)
    layer_out[...] = res_acc[...].astype(jnp.bfloat16)
    dh = dh_acc[...]
    grad_rows = e_ref[...].astype(jnp.float32)
    dx = grad_rows + norm_back(dh, unit, inverse, gain_two[...])
    dx_out[...] = dx
    da = dx.astype(jnp.bfloat16)
    da_out[...] = da
    do = dot(da, proj_w[...], NT).astype(jnp.bfloat16)
    do_out[...] = do
    product = do.astype(jnp.float32) * acc[...]
    delta = jnp.zeros((rows, LANES), jnp.float32)
    left = first_half()
    for p in range(HEADS // 2):
        here = product[:, p * LANES : (p + 1) * LANES]
        one = jnp.sum(jnp.where(left, here, 0.0), axis=1, keepdims=True)
        two = jnp.sum(jnp.where(left, 0.0, here), axis=1, keepdims=True)
        delta = jnp.where(column == 2 * p, one, delta)
        delta = jnp.where(column == 2 * p + 1, two, delta)
    stats_out[0] = log_total
    stats_out[1] = delta
    small_out[0:1] = jnp.sum(dh * unit, axis=0, keepdims=True)
    small_out[1:2] = jnp.sum(dh, axis=0, keepdims=True)
    small_out[2:3] = jnp.sum(grad_rows, axis=0, keepdims=True)
    small_out[3:4] = jnp.sum(da.astype(jnp.float32), axis=0, keepdims=True)

    side_copy(x_ref, z).wait_send()

    @pl.when(has_up)
    def _():
        up_copy(x_ref, z).wait_send()

    @pl.when(has_down)
    def _():
        down_copy(x_ref, z).wait_send()

    def sent(d, carry):
        @pl.when(z >= d)
        def _():
            side_copy(x_ref, z - d).wait_send()

            @pl.when(has_up)
            def _():
                up_copy(x_ref, z - d).wait_send()

        @pl.when(z + d < nz)
        def _():
            side_copy(x_ref, z + d).wait_send()

            @pl.when(has_down)
            def _():
                down_copy(x_ref, z + d).wait_send()

        return carry

    lax.fori_loop(1, nz, sent, 0)


def run_forward(x, e, ends, gain_one, shift_one, qkv_weight, qkv_bias, proj_weight, proj_bias, gain_two, shift_two, up_weight, up_bias, down_weight, down_bias, peers):
    rows, width = x.shape
    hidden = up_weight.shape[1]
    nz = peers // 2
    bf, f32 = jnp.bfloat16, jnp.float32
    vmem = pl.BlockSpec(memory_space=pltpu.VMEM)
    smem = pl.BlockSpec(memory_space=pltpu.SMEM)
    hbm = pl.BlockSpec(memory_space=pl.ANY)
    dma = pltpu.SemaphoreType.DMA
    outs = [
        ((rows, width), bf), ((peers * rows, width), bf), ((rows, width), bf), ((rows, width), bf), ((rows, width), bf),
        ((rows, width), bf), ((rows, width), bf), ((rows, hidden), bf), ((rows, hidden), bf), ((rows, width), f32),
        ((2, rows, LANES), f32), ((4 + hidden // width, width), f32),
    ]
    row = lambda v: v.reshape(1, -1)
    return pl.pallas_call(
        functools.partial(forward_kernel, nz, ends.shape[0]),
        out_shape=[jax.ShapeDtypeStruct(*o) for o in outs],
        in_specs=[vmem, vmem, smem] + [vmem] * 8 + [hbm] * 4,
        out_specs=[vmem] * len(outs),
        scratch_shapes=[
            pltpu.VMEM((peers * rows, width), bf),
            pltpu.VMEM(qkv_weight.shape, bf),
            pltpu.VMEM(proj_weight.shape, bf),
            pltpu.VMEM(up_weight.shape, bf),
            pltpu.VMEM(down_weight.shape, bf),
            pltpu.VMEM((2 * rows, 2 * width), bf),
            pltpu.VMEM((2 * rows, 2 * rows), f32),
            pltpu.VMEM((HEADS // 2, 2 * rows, LANES), f32),
            pltpu.VMEM((HEADS // 2, 2 * rows, LANES), f32),
            pltpu.VMEM((rows, width), f32),
            pltpu.VMEM((HEADS // 2, 2 * rows, LANES), bf),
            pltpu.VMEM((rows, width), f32),
            pltpu.VMEM((rows, width), f32),
            dma((nz,)), dma((nz,)), dma((nz,)), dma((nz,)), dma((nz,)), dma((nz,)), dma((4,)),
        ],
        compiler_params=pltpu.CompilerParams(collective_id=0, has_side_effects=True, vmem_limit_bytes=60 * 2**20),
        cost_estimate=pl.CostEstimate(flops=10**9, bytes_accessed=2 * 10**7, transcendentals=10**6),
    )(x, e, ends, row(gain_one), row(shift_one), row(qkv_bias), row(proj_bias), row(gain_two), row(shift_two), row(up_bias),
      row(down_bias), qkv_weight, proj_weight, up_weight, down_weight)


def backward_kernel(
    nz, items, orders,
    x_ref, e_ref, ends, gain_one, qkv_bias, n1_all, q_ref, attn_ref, da_ref, do_ref, n2_ref, g_ref, du_ref, dx_ref,
    stats_ref, first_small, qkv_hbm,
    input_grad, qkv_out, proj_out, up_out, down_out, small_out,
    qkv_w, buf, inbox, total, do_all, rows_all, g_cat, e_cat, n2_cat, du_cat, attn_cat, da_cat, n1_cat, dqkv_cat,
    two_q, two_do, two_k, two_v, lse_cols, delta_cols, kv, n1_held, mask, dq, dk, dv, small_in,
    down_send, down_recv, side_send, side_recv, ssem, rsem, lsem,
):
    rows, width = x_ref.shape
    pair = 2 * rows
    place = Place()
    seq, batch = place.seq, place.batch
    z = seq // 2
    x = seq % 2
    core = place.bit(CORE)
    sems = Sems(ssem, rsem)
    local = Sems(lsem, lsem)
    load = pltpu.make_async_copy(qkv_hbm, qkv_w, local.take()[0])
    load.start()
    small_axes = [CORE, ACROSS] + seq_axes(2 * nz)
    has_up = z + 1 < nz
    has_down = z > 0
    above = (seq + 2, batch)
    below = (seq - 2, batch)
    beside = (seq + 1 - 2 * x, batch)
    barrier = pltpu.get_barrier_semaphore()
    for axis in small_axes:
        pl.semaphore_signal(barrier, inc=1, device_id=place.partner(axis), device_id_type=MESH_ID)

    @pl.when(has_up)
    def _():
        pl.semaphore_signal(barrier, inc=1, device_id=above, device_id_type=MESH_ID)

    @pl.when(has_down)
    def _():
        pl.semaphore_signal(barrier, inc=1, device_id=below, device_id_type=MESH_ID)

    for k in range(2):
        rows_all[seq, k * TILE : (k + 1) * TILE] = stats_ref[k].T[:TILE]
    pl.semaphore_wait(barrier, len(small_axes) + has_up.astype(jnp.int32) + has_down.astype(jnp.int32))

    def cols(half, size):
        return pl.ds(pl.multiple_of(half * size, LANES), size)

    def to_core(source, into):
        return pltpu.make_async_remote_copy(
            source, into.at[rows:], *sems.take(), device_id=place.partner(CORE), device_id_type=MESH_ID
        )

    def keep_own(source, into):
        return pltpu.make_async_copy(source, into.at[:rows], local.take()[0])

    def exchange(ref, into, halved):
        size = into.shape[1]
        give = ref.at[:, cols(1 - core, size)] if halved else ref
        keep = ref.at[:, cols(core, size)] if halved else ref
        copies = [to_core(give, into), keep_own(keep, into)]
        for copy in copies:
            copy.start()
        return copies

    def done(copies):
        for copy in copies:
            copy.wait()

    down_parts = exchange(g_ref, g_cat, True) + exchange(e_ref, e_cat, False)
    up_parts = exchange(n2_ref, n2_cat, False) + exchange(du_ref, du_cat, True)

    def do_block(level, side):
        return do_all.at[rows_at((2 * level + side) * rows, rows)]

    def do_copies(level, side, to, send_sem, recv_sem, own=False):
        source = do_ref if own else do_block(level, side)
        stat = rows_all.at[2 * level + side]
        return [
            pltpu.make_async_remote_copy(
                source, do_block(level, side), send_sem.at[level, 0], recv_sem.at[level, 0], device_id=to, device_id_type=MESH_ID
            ),
            pltpu.make_async_remote_copy(
                stat, stat, send_sem.at[level, 1], recv_sem.at[level, 1], device_id=to, device_id_type=MESH_ID
            ),
        ]

    def down_copies(level, own=False):
        return do_copies(level, x, below, down_send, down_recv, own)

    def side_copies(level, own=False):
        return do_copies(level, x, beside, side_send, side_recv, own)

    def begin(copies):
        for copy in copies:
            copy.start()

    @pl.when(has_down)
    def _():
        begin(down_copies(z, True))

    begin(side_copies(z, True))
    do_all[rows_at(seq * rows, rows)] = do_ref[...]

    spread = [1]

    def spread_until(last):
        while spread[0] <= min(last, nz - 1):
            d = spread[0]
            spread[0] += 1

            @pl.when(z + d < nz)
            def _():
                level = z + d
                for copy in down_copies(level):
                    copy.wait_recv()

                @pl.when(has_down)
                def _():
                    begin(down_copies(level))

                begin(side_copies(level))

    def spread_end():
        def sent(copies):
            for copy in copies:
                copy.wait_send()

        sent(side_copies(z, True))

        @pl.when(has_down)
        def _():
            sent(down_copies(z, True))

        def each(level, carry):
            sent(side_copies(level))

            @pl.when(has_down)
            def _():
                sent(down_copies(level))

            return carry

        lax.fori_loop(z + 1, nz, each, 0)

    slots = []
    at = used = 0
    for size, kind, _ in items:
        slots.append((at, size, orders[kind], used))
        at += size
        used += sum(part for part, _ in parts_of(size, len(orders[kind])))
    places = [(name, r) for _, _, (name, r) in items]

    def destination(name, r, size):
        half = width // 2
        if name == "down":
            return down_out.at[rows_at(core * down_out.shape[0] // 2 + r, size)]
        if name[:2] == "up":
            return up_out.at[r : r + size, pl.ds(pl.multiple_of((core * (up_out.shape[1] // width // 2) + int(name[2:])) * width, width), width)]
        if name == "proj":
            return proj_out.at[rows_at(core * half + r, size)]
        return qkv_out.at[rows_at(core * half + r, size), int(name[3:]) * width : (int(name[3:]) + 1) * width]

    def item_task(k):
        at, size, order, used = slots[k]
        yield from sum_item(place, sems, buf, at, size, order, inbox, used, total)
        there = destination(*places[k], size)
        here = total.at[rows_at(at, size)]
        keep = pltpu.make_async_copy(here, there, local.take()[0])
        give = pltpu.make_async_remote_copy(here, there, *sems.take(), device_id=place.partner(CORE), device_id_type=MESH_ID)
        keep.start()
        give.start()
        yield
        keep.wait()
        give.wait()

    def small_task(group):
        held = small_out.at[8 * group : 8 * group + 8]
        for k, axis in enumerate(small_axes):
            copy = pltpu.make_async_remote_copy(
                held, small_in.at[group, k], *sems.take(), device_id=place.partner(axis), device_id_type=MESH_ID
            )
            copy.start()
            yield
            copy.wait()
            held[...] += small_in[group, k]

    live = []

    def turn(pieces):
        for task in list(live):
            if pieces:
                pieces.step()
            try:
                next(task)
            except StopIteration:
                live.remove(task)

    def enter(task):
        next(task)
        live.append(task)

    def weight_items(name, left, right):
        for k, (where, r) in enumerate(places):
            if where == name:
                at, size, _, _ = slots[k]
                buf[at : at + size] = dot(left[:, r : r + size], right, TN).astype(jnp.bfloat16)
                enter(item_task(k))

    small_out[:8] = first_small[...]
    done(down_parts)
    weight_items("down", g_cat, e_cat[...])
    done(up_parts)
    for j in range(du_cat.shape[1] // width):
        weight_items(f"up{j}", n2_cat, du_cat[:, j * width : (j + 1) * width])
    proj_parts = exchange(attn_ref, attn_cat, True) + exchange(da_ref, da_cat, False)
    own_n1 = rows_at(seq * rows, rows)
    n1_parts = exchange(n1_all.at[own_n1], n1_cat, True)
    enter(small_task(0))

    load.wait()
    scale = jnp.asarray(1.0 / math.sqrt(HD), jnp.bfloat16)

    chunk_sem = local.take()[0]

    def n1_chunk(level):
        copy = pltpu.make_async_copy(n1_all.at[rows_at(level * pair, pair)], n1_held, chunk_sem)
        copy.start()
        copy.wait()
        return n1_held[...]

    def prepare():
        n1_chunk(z)
        mine = n1_held[rows_at(x * rows, rows)]
        own_kv = (dot(mine, qkv_w[:, width:]) + qkv_bias[:, width:]).astype(jnp.bfloat16)
        for p in range(HEADS // 2):
            here = slice(p * LANES, (p + 1) * LANES)
            two_q[p] = both_heads(q_ref[:, here])
            two_do[p] = both_heads(do_ref[:, here])
            two_k[p] = both_heads(own_kv[:, here])
            two_v[p] = both_heads(own_kv[:, width + p * LANES : width + (p + 1) * LANES])
            for k, into in enumerate((lse_cols, delta_cols)):
                for h in range(2):
                    column = stats_ref[k, :, 2 * p + h : 2 * p + h + 1]
                    into[p, h * rows : (h + 1) * rows] = jnp.broadcast_to(column, (rows, LANES))
        dq[...] = jnp.zeros(dq.shape, jnp.float32)
        dk[...] = jnp.zeros(dk.shape, jnp.float32)
        dv[...] = jnp.zeros(dv.shape, jnp.float32)

    def columns_of(p):
        return pl.ds(pl.multiple_of(p * LANES, LANES), LANES)

    def query_step(level):
        n1 = n1_chunk(level)
        kv[...] = (dot(n1, qkv_w[:, width:]) + qkv_bias[:, width:]).astype(jnp.bfloat16)
        one = mask_of(ends, places_down(seq * rows, rows), places_along(level * pair, pair))
        mask[:rows] = one
        mask[rows:] = one

        def each(p, carry):
            k_pair = kv[:, columns_of(p)]
            v_pair = kv[:, columns_of(p + HEADS // 2)]
            s = dot(two_q[p], k_pair, NT)
            along = dot(two_do[p], v_pair, NT)
            low = mask[...] - lse_cols[p][:, :1]
            plus = jnp.exp(low + s)
            minus = jnp.exp(low - s)
            ds = ((plus + minus) * along - (plus - minus) * delta_cols[p][:, :1]).astype(jnp.bfloat16)
            dq[:, columns_of(p)] += own_columns(dot(ds, k_pair))
            return carry

        lax.fori_loop(0, HEADS // 2, each, 0)

    def key_step(level):
        side = 1 - x
        for copy in do_copies(level, side, beside, side_send, side_recv):
            copy.wait_recv()
        here = rows_at(level * pair, pair)
        n1 = n1_chunk(level)
        kv[:, :width] = (dot(n1, qkv_w[:, :width]) + qkv_bias[:, :width]).astype(jnp.bfloat16) * scale
        one = mask_of(ends, places_along(level * pair, pair), places_down(seq * rows, rows))
        mask[:rows] = one
        mask[rows:] = one

        def stat(row):
            both = [rows_all[2 * level + k, pl.ds(row, 1)] for k in range(2)]
            return jnp.concatenate(both, axis=1)

        def stat_rows(k, p):
            both = [jnp.broadcast_to(stat(k * TILE + 2 * p + h), (rows, pair)) for h in range(2)]
            return jnp.concatenate(both, axis=0)

        def each(p, carry):
            q_pair = kv[:, columns_of(p)]
            do_pair = do_all[here, columns_of(p)]
            s = dot(two_k[p], q_pair, NT)
            along = dot(two_v[p], do_pair, NT)
            low = mask[...] - stat_rows(0, p)
            plus = jnp.exp(low + s)
            minus = jnp.exp(low - s)
            signed = plus - minus
            ds = ((plus + minus) * along - signed * stat_rows(1, p)).astype(jnp.bfloat16)
            dk[:, columns_of(p)] += own_columns(dot(ds, q_pair))
            dv[:, columns_of(p)] += own_columns(dot(signed.astype(jnp.bfloat16), do_pair))
            return carry

        lax.fori_loop(0, HEADS // 2, each, 0)

    def one_step(t):
        @pl.when(t <= z)
        def _():
            query_step(z - t)

        @pl.when(t > z)
        def _():
            key_step(t - 1)

    def steps_piece(first, last):
        def piece():
            spread_until(last)
            if last - first == 1:
                one_step(first)
            else:

                def body(t, carry):
                    one_step(t)
                    return carry

                lax.fori_loop(first, last, body, 0)

        return piece

    def proj_piece():
        done(proj_parts)
        weight_items("proj", attn_cat, da_cat[...])

    groups = min(nz + 1, GROUPS)
    cuts = [(nz + 1) * k // groups for k in range(groups + 1)]
    pieces = Paced([prepare, proj_piece] + [steps_piece(a, b) for a, b in zip(cuts, cuts[1:])], PACE)
    while pieces.left():
        turn(pieces)

    dqkv = jnp.concatenate(
        [
            (dq[...] * (1.0 / math.sqrt(HD))).astype(jnp.bfloat16),
            dk[...].astype(jnp.bfloat16),
            dv[...].astype(jnp.bfloat16),
        ],
        axis=1,
    )
    dqkv_cat[:rows] = dqkv
    send = to_core(dqkv_cat.at[:rows], dqkv_cat)
    send.start()
    dh = dot(dqkv, qkv_w[...], NT)
    unit, inverse = norm_parts(x_ref[...].astype(jnp.float32))
    input_grad[...] = (dx_ref[...] + norm_back(dh, unit, inverse, gain_one[...])).astype(jnp.bfloat16)
    sums = jnp.sum(dqkv.astype(jnp.float32), axis=0, keepdims=True)
    for k in range(3):
        small_out[8 + k : 9 + k] = sums[:, k * width : (k + 1) * width]
    small_out[11:12] = jnp.sum(dh * unit, axis=0, keepdims=True)
    small_out[12:13] = jnp.sum(dh, axis=0, keepdims=True)
    small_out[13:16] = jnp.zeros((3, width), jnp.float32)
    done(n1_parts)
    send.wait()
    for j in range(3):
        weight_items(f"qkv{j}", n1_cat, dqkv_cat[:, j * width : (j + 1) * width])
    enter(small_task(1))
    while live:
        turn(None)
    spread_end()


class Paced:
    def __init__(self, pieces, every):
        self.pieces, self.every, self.asked = pieces, every, 0

    def left(self):
        return len(self.pieces)

    def step(self):
        if self.pieces and self.asked % self.every == 0:
            self.pieces.pop(0)()
        self.asked += 1


def plan_items(width, hidden):
    half = width // 2

    def cut(name, size):
        return [(min(ITEM, size - r), (name, r)) for r in range(0, size, ITEM)]

    found = cut("down", hidden // 2)
    for j in range(hidden // 2 // width):
        found += cut(f"up{j}", width)
    found += cut("proj", half)
    for j in range(3):
        found += cut(f"qkv{j}", half)
    return [(size, int(KINDS[k % len(KINDS)]), where) for k, (size, where) in enumerate(found)]


def run_backward(x, e, ends, gain_one, qkv_weight, qkv_bias, kept, peers):
    n1_all, q, attn, da, do, n2, g, du, dx, stats, small = kept
    rows, width = x.shape
    hidden = g.shape[1]
    nz = peers // 2
    bf, f32 = jnp.bfloat16, jnp.float32
    orders = axis_orders(peers)
    items = plan_items(width, hidden)
    counts = [parts_of(size, len(orders[kind])) for size, kind, _ in items]
    used = sum(part for count in counts for part, _ in count)
    height = sum(size for size, _, _ in items)
    stages = 2 + len(seq_axes(peers))
    copies = sum(1 + len(count) + sum(halve for _, halve in count) for count in counts) + 2 * stages + 8
    vmem = pl.BlockSpec(memory_space=pltpu.VMEM)
    smem = pl.BlockSpec(memory_space=pltpu.SMEM)
    hbm = pl.BlockSpec(memory_space=pl.ANY)
    dma = pltpu.SemaphoreType.DMA
    row = lambda v: v.reshape(1, -1)
    out = jax.ShapeDtypeStruct
    stack = (HEADS // 2, 2 * rows, LANES)
    return pl.pallas_call(
        functools.partial(backward_kernel, nz, items, orders),
        out_shape=[
            out((rows, width), bf), out((width, 3 * width), bf), out((width, width), bf), out((width, hidden), bf),
            out((hidden, width), bf), out((16, width), f32),
        ],
        in_specs=[vmem, hbm, smem, vmem, vmem, hbm, vmem, hbm, hbm, vmem, hbm, hbm, hbm, vmem, vmem, vmem, hbm],
        out_specs=[vmem, hbm, hbm, hbm, hbm, vmem],
        scratch_shapes=[
            pltpu.VMEM(qkv_weight.shape, bf),
            pltpu.VMEM((height, width), bf),
            pltpu.VMEM((used, width), bf),
            pltpu.VMEM((height, width), bf),
            pltpu.VMEM((peers * rows, width), bf),
            pltpu.VMEM((peers, 2 * TILE, LANES), f32),
            pltpu.VMEM((2 * rows, hidden // 2), bf),
            pltpu.VMEM((2 * rows, width), bf),
            pltpu.VMEM((2 * rows, width), bf),
            pltpu.VMEM((2 * rows, hidden // 2), bf),
            pltpu.VMEM((2 * rows, width // 2), bf),
            pltpu.VMEM((2 * rows, width), bf),
            pltpu.VMEM((2 * rows, width // 2), bf),
            pltpu.VMEM((2 * rows, 3 * width), bf),
            pltpu.VMEM(stack, bf), pltpu.VMEM(stack, bf), pltpu.VMEM(stack, bf), pltpu.VMEM(stack, bf),
            pltpu.VMEM(stack, f32), pltpu.VMEM(stack, f32),
            pltpu.VMEM((2 * rows, 2 * width), bf),
            pltpu.VMEM((2 * rows, width), bf),
            pltpu.VMEM((2 * rows, 2 * rows), f32),
            pltpu.VMEM((rows, width), f32), pltpu.VMEM((rows, width), f32), pltpu.VMEM((rows, width), f32),
            pltpu.VMEM((2, stages, 8, width), f32),
            dma((nz, 2)), dma((nz, 2)), dma((nz, 2)), dma((nz, 2)),
            dma((copies,)), dma((copies,)), dma((len(items) + 10,)),
        ],
        compiler_params=pltpu.CompilerParams(collective_id=1, has_side_effects=True, vmem_limit_bytes=62 * 2**20),
    )(x, e, ends, row(gain_one), row(qkv_bias), n1_all, q, attn, da, do, n2, g, du, dx, stats, small, qkv_weight)


def per_device(
    inputs,
    cotangent,
    doc_lengths,
    gain_one,
    shift_one,
    qkv_weight,
    qkv_bias,
    proj_weight,
    proj_bias,
    gain_two,
    shift_two,
    up_weight,
    up_bias,
    down_weight,
    down_bias,
):
    peers = lax.axis_size("seq")
    width = inputs.shape[2]
    ends = running_sum(doc_lengths[0])
    layer_out, *kept = run_forward(
        inputs[0], cotangent[0], ends, gain_one, shift_one, qkv_weight, qkv_bias, proj_weight, proj_bias, gain_two, shift_two,
        up_weight, up_bias, down_weight, down_bias, peers,
    )
    input_grad, qkv, proj, up, down, small = run_backward(
        inputs[0], cotangent[0], ends, gain_one, qkv_weight, qkv_bias, kept, peers
    )
    wide = jnp.float32
    return (
        layer_out[None],
        input_grad[None],
        small[11],
        small[12],
        qkv.astype(wide),
        small[8:11].reshape(-1),
        proj.astype(wide),
        small[3],
        small[0],
        small[1],
        up.astype(wide),
        small[4:8].reshape(-1),
        down.astype(wide),
        small[2],
    )


def solution(mesh):
    in_specs = (
        P("batch", "seq", None),
        P("batch", "seq", None),
        P("batch", None),
        P(),
        P(),
        P(),
        P(),
        P(),
        P(),
        P(),
        P(),
        P(),
        P(),
        P(),
        P(),
    )
    out_specs = (
        P("batch", "seq", None),
        P("batch", "seq", None),
        P(),
        P(),
        P(),
        P(),
        P(),
        P(),
        P(),
        P(),
        P(),
        P(),
        P(),
        P(),
    )
    return jax.shard_map(
        per_device, mesh=mesh, in_specs=in_specs, out_specs=out_specs, check_vma=False
    )
```

time: 1440 us -> 222 us (0.15)
  blocking collectives: 458 us -> 0 us
  waiting for transfers between devices: 358 us -> 0 us
  local copies, waits for them, and re-layouts: 299 us -> 12.2 us
  Pallas kernels: 0 us -> 190 us
  matrix products: 131 us -> 0 us
  other arithmetic: 106 us -> 18.3 us
  starting transfers between devices: 58.3 us -> 0 us
    unnamed x1 -> x0, blocking collectives: 458 us -> none
    unnamed x4 -> x0, waiting for transfers between devices: 243 us -> none
    pallas_call x0 -> x2, Pallas kernels: none -> 190 us  [the longest x1 155 us: run_backward(): pl.pallas_call(functools.partial(backward_kernel, nz, items, orders), out...]
    unnamed x123 -> x14, local copies, waits for them, and re-layouts: 133 us -> 1.38 us
    dot_general x68 -> x0, matrix products: 131 us -> none  [the longest x16 33.6 us: scores_of(): jnp.einsum('qhd,khd->hqk', q_heads, k_heads, preferred_element_type=jnp.f...]
    all_gather x2 -> x0, waiting for transfers between devices: 84.5 us -> none  [the longest x1 45.8 us: per_device(): v_all = lax.all_gather(v_flat, 'seq', axis=0, tiled=True)]
    ppermute x32 -> x0, starting transfers between devices: 58.2 us -> none  [the longest x16 41.9 us: from_behind(): return lax.ppermute(shard, axis, pairs)]
    dynamic_slice x32 -> x0, local copies, waits for them, and re-layouts: 52.1 us -> none  [the longest x16 28.3 us: one(): v_blk = lax.dynamic_slice_in_dim(v_all, offset, rows, 0)]
  transfers between devices with their start and end apart: 35 -> 0, of which waited for: 19 -> 0; matrix products, arithmetic and copies ran while one was open for 9% -> 0% of each run, Pallas kernels for 0% -> 0%
where the time goes in v2:
time: 222 us; the launch traced here: 221 us
  Pallas kernels  190 us (86%)
  other arithmetic  18.3 us (8%)
  local copies, waits for them, and re-layouts  12.2 us (5%)
    pallas_call x1, Pallas kernels, run_backward(): pl.pallas_call(functools.partial(backward_kernel, nz, items, orders), out...  155 us
    pallas_call x1, Pallas kernels, run_forward(): pl.pallas_call(functools.partial(forward_kernel, nz, ends.shape[0]), out_...  35 us
    reshape x7, local copies, waits for them, and re-layouts, run_forward(): row = lambda v: v.reshape(1, -1)  8.91 us
    convert_element_type x1, other arithmetic, per_device(): up.astype(wide)  7.52 us
    convert_element_type x1, other arithmetic, per_device(): down.astype(wide)  4.48 us

profile of v2, /device:TPU:0, one launch (start us, length us, event | category | flops | bytes accessed | tf_op | source)
XLA Modules:
  0.0 221.5 jit_solution(14118719778591555861)
XLA Ops:
  0.6 1.3 reshape.62.qkv_bias
  2.0 1.3 reshape.60.gain_one
  3.2 1.3 select_reduce_fusion.ends
  4.5 1.3 reshape.61.shift_one
  5.8 1.3 reshape.63.proj_bias
  7.0 1.3 reshape.64.gain_two
  8.3 1.3 reshape.65.shift_two
  9.6 1.3 reshape.67.down_bias
  10.8 35.0 %shard_map.254 = (bf16[128,768]{1,0:T(8,128)(2,1)}, bf16[1024,768]{1,0:T(8,128)(2,1)}, bf16[128,768]{1,0:T(8,128)(2,1)}, bf16[128,768]{1,0:T(8,128)(2,1)}, bf16[...) custom-call(bf16[128,768]{1,0:T(8,128)(2,1)} %bitcast.6, ...), custom_call_target="tpu_custom_call" | custom-call | flops 1000000000 | bytes 20000000 | tf_op jit(solution)/shard_map/pallas_call | solution.py:464
  45.8 155.3 %shard_map.255 = (bf16[128,768]{1,0:T(8,128)(2,1)}, bf16[768,2304]{1,0:T(8,128)(2,1)}, bf16[768,768]{1,0:T(8,128)(2,1)}, bf16[768,3072]{1,0:T(8,128)(2,1)}, bf16...) custom-call(bf16[128,768]{1,0:T(8,128)(2,1)} %bitcast.7, bf16[128,768]{1,0:T(8,128)(2,1)} %bitcast.9, s32[9]{0:T(128)} %select_reduce_fusion.ends, ...), custom_call_target="tpu_custom_call" | custom-call | tf_op jit(solution)/shard_map/pallas_call | solution.py:908
  201.2 0.0 copy-start
  201.2 7.5 %convert_element_type.14 = f32[768,3072]{1,0:T(8,128)} convert(bf16[768,3072]{1,0:T(8,128)(2,1)} %get-tuple-element.48) | non-fusion elementwise | flops 2359296 | bytes 14155776 | tf_op jit(solution)/shard_map/convert_element_type | solution.py:984
  208.7 0.0 copy-done
  208.7 0.0 copy-start.1
  208.7 4.5 %convert_element_type.15 = f32[3072,768]{1,0:T(8,128)} convert(bf16[3072,768]{1,0:T(8,128)(2,1)S(1)} %copy-done) | non-fusion elementwise | flops 2359296 | bytes 14155776 | tf_op jit(solution)/shard_map/convert_element_type | solution.py:986
  213.2 0.0 copy-done.1
  213.2 0.0 copy-start.2
  213.2 0.0 copy-start.5
  213.2 0.0 copy-start.3
  213.2 0.0 copy-start.4
  213.2 3.5 %convert_element_type.12 = f32[768,2304]{1,0:T(8,128)} convert(bf16[768,2304]{1,0:T(8,128)(2,1)S(1)} %copy-done.1) | non-fusion elementwise | flops 1769472 | bytes 10616832 | tf_op jit(solution)/shard_map/convert_element_type | solution.py:978
  216.7 0.0 copy-done.2
  216.7 1.6 convert_element_type.13
  218.3 0.0 copy-done.5
  218.3 0.6 slice_reduce_fusion
  218.9 0.6 reshape.68
  219.5 0.6 reshape.69
  220.1 0.0 copy-done.3
  220.1 0.7 copy.31
  220.8 0.0 copy-done.4
  220.8 0.7 copy.32
  (2 shorter events, 0.0 us)
Async XLA Ops:
  201.2 7.5 %copy-start = (bf16[3072,768]{1,0:T(8,128)(2,1)S(1)}, bf16[3072,768]{1,0:T(8,128)(2,1)}, u32[]{:S(2)}) copy-start(bf16[3072,768]{1,0:T(8,128)(2,1)} %get-tuple-element.49) | copy-start | bytes 14155780
  208.7 4.5 %copy-start.1 = (bf16[768,2304]{1,0:T(8,128)(2,1)S(1)}, bf16[768,2304]{1,0:T(8,128)(2,1)}, u32[]{:S(2)}) copy-start(bf16[768,2304]{1,0:T(8,128)(2,1)} %get-tuple-element.46) | copy-start | bytes 10616836
  213.2 3.5 %copy-start.2 = (bf16[768,768]{1,0:T(8,128)(2,1)S(1)}, bf16[768,768]{1,0:T(8,128)(2,1)}, u32[]{:S(2)}) copy-start(bf16[768,768]{1,0:T(8,128)(2,1)} %get-tuple-element.47) | copy-start | bytes 3538948
  213.2 5.1 %copy-start.5 = (f32[16,768]{1,0:T(8,128)S(1)}, f32[16,768]{1,0:T(8,128)}, u32[]{:S(2)}) copy-start(f32[16,768]{1,0:T(8,128)} %get-tuple-element.45) | copy-start | bytes 147460
  213.2 7.0 %copy-start.3 = (bf16[128,768]{1,0:T(8,128)(2,1)S(1)}, bf16[128,768]{1,0:T(8,128)(2,1)}, u32[]{:S(2)}) copy-start(bf16[128,768]{1,0:T(8,128)(2,1)} %get-tuple-element.32) | copy-start | bytes 589828
  213.2 7.6 %copy-start.4 = (bf16[128,768]{1,0:T(8,128)(2,1)S(1)}, bf16[128,768]{1,0:T(8,128)(2,1)}, u32[]{:S(2)}) copy-start(bf16[128,768]{1,0:T(8,128)(2,1)} %get-tuple-element.44) | copy-start | bytes 589828
